TPU v7x, 32 devices: a whole 2x2x4 slice. The times are simulated.
32 devices in a mesh: vec: 4 (over y, x), gz: 8 (over z, core).
Axes of the slice: x: 2, y: 2, z: 4, core: 2. Of those that a mesh axis runs over, the one named last changes fastest.
Arguments:
- vectors: bfloat16 [1024, 3, 2, 4096], P('vec', None, None, 'gz'), may hold values from -6 to 6
- links: float32 [3, 3, 3, 2, 4096], P(None, None, None, None, 'gz'), may hold values from -4 to 4
- dirs: int32 [6], replicated, may hold values from 0 to 5, each once
- moms: int32 [2, 3], replicated, may hold values from -2 to 2
Outputs:
- elementals: float32 [6, 2, 2, 1024, 1024], P(None, None, None, ('vec', 'gz'))
Inputs may be any that keep to these rules, and one draw needn't show every extreme that they name: `dirs`: each of the six directions appears exactly once.
All inputs are finite; a program needn't handle non-finite values.
Results may differ from a plain program's by a relative error of at most 0.0039.
Values may be sent and summed in bfloat16 or wider, within the bound.
No kernel may reach another device: no remote copies, remote signals or barrier semaphores. Data moves between devices by JAX's collectives and lax.ppermute only.
A program may use at most 192 MiB of HBM per device.

v0:
```python
import functools
import math

import jax
import jax.numpy as jnp
from jax import lax
from jax.experimental import pallas as pl
from jax.experimental.pallas import tpu as pltpu
from jax.sharding import PartitionSpec as P

LX = 32
LY = 8
PLANE = LX * LY
LANES = 128
CORES = 2
VMEM_BYTES = 48 * 1024 * 1024
COST_SCALE = 1.0


def cost(work):
    return pl.CostEstimate(flops=int(work * COST_SCALE), bytes_accessed=1024, transcendentals=0)


def shifted(chunks, axis, sign):
    lane = lax.broadcasted_iota(jnp.int32, chunks[0].shape, 1)
    if axis == 0:
        near = LANES - 1 if sign > 0 else 1
        far = LX - 1 if sign > 0 else LANES - (LX - 1)
        edge = lax.rem(lane, LX) == (LX - 1 if sign > 0 else 0)
        return [jnp.where(edge, pltpu.roll(c, far, 1), pltpu.roll(c, near, 1)) for c in chunks]
    turned = [pltpu.roll(c, LANES - LX if sign > 0 else LX, 1) for c in chunks]
    inside = lane < LANES - LX if sign > 0 else lane >= LX
    count = len(chunks)
    return [jnp.where(inside, turned[n], turned[(n + sign) % count]) for n in range(count)]


def apply_link(moved, link, adjoint):
    for row in range(3):
        real = imag = None
        for column in range(3):
            link_real, link_imag = link(column, row) if adjoint else link(row, column)
            vec_real, vec_imag = moved[2 * column], moved[2 * column + 1]
            if adjoint:
                terms = (link_real * vec_real + link_imag * vec_imag, link_real * vec_imag - link_imag * vec_real)
            else:
                terms = (link_real * vec_real - link_imag * vec_imag, link_real * vec_imag + link_imag * vec_real)
            real, imag = terms if real is None else (real + terms[0], imag + terms[1])
        yield row, real, imag


def store_left(out_ref, base, slab, axis, sign_at, first, moved, link, phase_ref, momenta, rows, sites):
    lanes = pl.ds(first, LANES)
    for row, real, imag in apply_link(moved, link, sign_at == 0):
        for p in range(momenta):
            at = ((slab * 3 + axis) * 2 + sign_at) * momenta + p
            cosine = phase_ref[0, pl.ds(at, 1), lanes]
            sine = phase_ref[1, pl.ds(at, 1), lanes]
            down = pl.ds(base + (sign_at * momenta + p) * rows, rows)
            column = row * 2 * sites + first
            out_ref[0, down, pl.ds(column, LANES)] = (cosine * real - sine * imag).astype(jnp.bfloat16)
            out_ref[0, down, pl.ds(column + sites, LANES)] = (sine * real + cosine * imag).astype(jnp.bfloat16)


def phase_kernel(momenta, sites, extents, place_ref, moms_ref, out_ref, angles):
    flat = lax.broadcasted_iota(jnp.int32, (1, sites), 1)
    depth = sites // PLANE
    turns = [[moms_ref[p, mu].astype(jnp.float32) / extents[mu] for mu in range(3)] for p in range(momenta)]
    at = 0
    for slab in range(2):
        core = place_ref[1] if slab == 0 else 1 - place_ref[1]
        planes = flat // PLANE + (place_ref[0] * CORES + core) * depth
        coordinates = [c.astype(jnp.float32) for c in (lax.rem(flat, LX), lax.rem(flat // LX, LY), planes)]
        base = [sum(turns[p][mu] * coordinates[mu] for mu in range(3)) for p in range(momenta)]
        for axis in range(3):
            for sign in (-1.0, 1.0):
                for p in range(momenta):
                    angles[pl.ds(at, 1), :] = (base[p] + sign * turns[p][axis]) * (2.0 * math.pi)
                    at += 1
    out_ref[0] = jnp.cos(angles[...])
    out_ref[1] = jnp.sin(angles[...])


def edge_kernel(sites, place_ref, same_ref, cross_ref, same_out, cross_out):
    for ref, out in ((same_ref, same_out), (cross_ref, cross_out)):
        for c in range(6):
            lowest = ref[:, pl.ds(c * sites, PLANE)]
            highest = ref[:, pl.ds((c + 1) * sites - PLANE, PLANE)]
            out[:, pl.ds(c * PLANE, PLANE)] = jnp.where(place_ref[1] == 0, lowest, highest)


def left_xy_kernel(momenta, rows, sites, slab, place_ref, vec_ref, link_ref, phase_ref, out_ref, table):
    chunks = PLANE // LANES
    for axis in range(2):
        for plane in range(sites // PLANE):
            starts = [plane * PLANE + n * LANES for n in range(chunks)]
            behind = shifted([link_ref[axis, :, pl.ds(at, LANES)] for at in starts], axis, -1)
            for n in range(chunks):
                table[:, pl.ds(n * LANES, LANES)] = behind[n]
            parts = [[vec_ref[:, pl.ds(c * sites + at, LANES)].astype(jnp.float32) for at in starts] for c in range(6)]
            for sign_at, sign in enumerate((-1, 1)):
                moved = [shifted(part, axis, sign) for part in parts]
                for n, at in enumerate(starts):
                    if sign_at == 0:
                        source = lambda row, n=n: table[pl.ds(row, 1), pl.ds(n * LANES, LANES)]
                    else:
                        source = lambda row, at=at: link_ref[axis, pl.ds(row, 1), pl.ds(at, LANES)]
                    link = lambda a, b, source=source: (source((a * 3 + b) * 2), source((a * 3 + b) * 2 + 1))
                    store_left(
                        out_ref, axis * 2 * momenta * rows, slab, axis, sign_at, at, [m[n] for m in moved], link,
                        phase_ref, momenta, rows, sites,
                    )


def left_z_kernel(
    momenta, rows, sites, place_ref, own_ref, other_ref, first_ref, second_ref, link_ref, other_link_ref, phase_ref,
    *refs,
):
    low = place_ref[1] == 0
    top = sites - PLANE
    read = lambda ref, c, at: ref[:, pl.ds(c + at, LANES)].astype(jnp.float32)
    for slab in range(2):
        mine, theirs = (own_ref, other_ref) if slab == 0 else (other_ref, own_ref)
        links = link_ref if slab == 0 else other_link_ref
        below_is_halo = low if slab == 0 else jnp.logical_not(low)
        halo = second_ref if slab == 0 else first_ref
        for at in range(0, sites, LANES):
            for sign_at, sign in enumerate((-1, 1)):
                source = at + sign * PLANE
                if 0 <= source < sites:
                    moved = [read(mine, c * sites, source) for c in range(6)]
                elif source < 0:
                    moved = [
                        jnp.where(below_is_halo, read(halo, c * PLANE, at), read(theirs, c * sites, top + at))
                        for c in range(6)
                    ]
                else:
                    moved = [
                        jnp.where(below_is_halo, read(theirs, c * sites, at - top), read(halo, c * PLANE, at - top))
                        for c in range(6)
                    ]
                kind = 3 if sign_at == 0 else 2
                value = lambda row, kind=kind, at=at: links[kind, pl.ds(row, 1), pl.ds(at, LANES)]
                link = lambda a, b, value=value: (value((a * 3 + b) * 2), value((a * 3 + b) * 2 + 1))
                store_left(refs[2 + slab], 0, slab, 2, sign_at, at, moved, link, phase_ref, momenta, rows, sites)


def product_kernel(sites, half, first_row, size, parts, received, targets, *refs):
    mine, theirs = refs[:parts], refs[parts : 2 * parts]
    left = refs[2 * parts : 2 * parts + 2]
    got = refs[2 * parts + 2 : 2 * parts + 2 + received]
    *outs, right, rows, right_sems, left_sems = refs[2 * parts + 2 + received :]
    width = right.shape[0] // 2
    span = 6 * sites
    columns = [pl.ds(slab * span, span) for slab in range(2)]
    copies = [[], []]
    for slab, pieces in enumerate((mine, theirs)):
        start = 0
        for n, piece in enumerate(pieces):
            count = piece.shape[0]
            copies[slab].append(
                pltpu.make_async_copy(piece, right.at[pl.ds(start, count), columns[slab]], right_sems.at[slab, n])
            )
            start += count
        for n in range(half):
            copies[slab].append(
                pltpu.make_async_copy(
                    left[slab].at[n, pl.ds(first_row, size)], rows.at[pl.ds(n * size, size), columns[slab]],
                    left_sems.at[slab, n],
                )
            )
    for slab in range(2):
        for copy in copies[slab]:
            copy.start()
    sums = None
    for slab in range(2):
        for copy in copies[slab]:
            copy.wait()
        for colour in range(3):
            real_at = slab * span + 2 * colour * sites
            imag_at = real_at + sites
            right[pl.ds(width, width), pl.ds(real_at, sites)] = right[pl.ds(0, width), pl.ds(imag_at, sites)]
            right[pl.ds(width, width), pl.ds(imag_at, sites)] = -right[pl.ds(0, width), pl.ds(real_at, sites)]
        part = lax.dot_general(
            rows[:, columns[slab]], right[:, columns[slab]], (((1,), (1,)), ((), ())),
            preferred_element_type=jnp.float32,
        )
        sums = part if sums is None else sums + part
    for n, (which, place) in enumerate(targets):
        for q in range(2):
            total = sums[n * size : (n + 1) * size, q * width : (q + 1) * width]
            if not got:
                outs[which][place, q] = total.astype(outs[which].dtype)
            start = 0
            for ref in got:
                count = ref.shape[2]
                added = total[start : start + count] + ref[n, q].astype(jnp.float32)
                outs[which][place, q, pl.ds(start, count)] = added.astype(outs[which].dtype)
                start += count


def finish_kernel(pieces, momenta, rows, scale, place_ref, *refs):
    out_ref = refs[-1]
    size = momenta * rows
    for d in range(6):
        at = pl.ds(pl.multiple_of(place_ref[d] * size, size), size)
        for q in range(2):
            total = refs[0][0, q, at].astype(jnp.float32)
            for ref in refs[1:pieces]:
                total = total + ref[0, q, at].astype(jnp.float32)
            total = total * scale
            for p in range(momenta):
                out_ref[d, p, q] = total[p * rows : (p + 1) * rows]


def after(value, *earlier):
    return lax.optimization_barrier((value, *earlier))[0]


def order(last):
    steps = [("left", (1, 0)), ("left", (1, 1)), ("xy", 0), ("pass", 1), ("left_z", 1), ("z", 0)]
    steps += [("left", (0, 0)), ("left", (0, 1)), ("pass", 2), ("left_z", 0)]
    for n in range(max(last, 1)):
        if n + 1 < last:
            steps.append(("away", n + 1))
        elif n + 1 == last:
            steps += [("direct", 1), ("direct", 0)]
        steps.append(("home", n))
        if n > 0:
            steps.append(("finish", n - 1))
        if n + 1 < last:
            steps += [("pass", n + 3)] if n + 3 <= last else []
    return steps + [("finish", n) for n in range(max(last - 1, 0), last + 1)]


def on_device(vectors, links, dirs, moms):
    count, sites = vectors.shape[0], vectors.shape[-1]
    momenta = moms.shape[0]
    groups, slabs = lax.axis_size("vec"), lax.axis_size("gz")
    chips = slabs // CORES
    half = chips // 2
    rows = count // slabs
    depth = sites // PLANE
    span = 6 * sites
    group, slab = lax.axis_index("vec"), lax.axis_index("gz")
    core, chip = slab % CORES, slab // CORES
    place = jnp.stack((chip, core)).astype(jnp.int32)
    across = [(i, i ^ 1) for i in range(slabs)]
    params = pltpu.CompilerParams(vmem_limit_bytes=VMEM_BYTES)

    link_rows = links.reshape(3, 18, sites)
    top = link_rows[2, :, sites - PLANE :]
    other_links = lax.ppermute(link_rows, "gz", across)
    below = lax.ppermute(top, "gz", [(i, (i + 1) % slabs) for i in range(slabs)])
    two_below = lax.ppermute(top, "gz", [(i, (i + 2) % slabs) for i in range(slabs)])

    def with_shifted(link, lower):
        moved = jnp.concatenate((lower, link[2, :, : sites - PLANE]), axis=-1)
        return jnp.concatenate((link, moved[None]), axis=0)

    tables = with_shifted(link_rows, below)
    other_tables = with_shifted(other_links, jnp.where(core == 0, top, two_below))

    flat = after(vectors.reshape(count, span), other_links, below, two_below)
    other = lax.ppermute(flat, "gz", across)

    edge_shape = jax.ShapeDtypeStruct((chips * rows, 6 * PLANE), jnp.bfloat16)
    same, cross = pl.pallas_call(
        functools.partial(edge_kernel, sites),
        grid_spec=pltpu.PrefetchScalarGridSpec(
            num_scalar_prefetch=1,
            grid=(chips,),
            in_specs=[
                pl.BlockSpec((rows, span), lambda n, place: (n * CORES + place[1], 0)),
                pl.BlockSpec((rows, span), lambda n, place: (n * CORES + 1 - place[1], 0)),
            ],
            out_specs=[pl.BlockSpec((rows, 6 * PLANE), lambda n, place: (n, 0))] * 2,
        ),
        out_shape=[edge_shape] * 2,
        compiler_params=params,
        cost_estimate=cost(1e9),
        name="edges",
    )(place, flat, flat)
    step = lambda i: (i - CORES if i % CORES == 0 else i + CORES) % slabs
    first = lax.ppermute(same, "gz", [(i, step(i)) for i in range(slabs)])
    second = lax.ppermute(cross, "gz", [(i, step(i) ^ 1) for i in range(slabs)])

    phase_rows = 2 * 3 * 2 * momenta
    phases = pl.pallas_call(
        functools.partial(phase_kernel, momenta, sites, (LX, LY, depth * slabs)),
        in_specs=[pl.BlockSpec(memory_space=pltpu.SMEM)] * 2,
        out_shape=jax.ShapeDtypeStruct((2, phase_rows, sites), jnp.float32),
        scratch_shapes=[pltpu.VMEM((phase_rows, sites), jnp.float32)],
        compiler_params=params,
        cost_estimate=cost(1e9),
        name="phases",
    )(place, moms)

    left_rows = 6 * momenta * rows
    whole = lambda array: pl.BlockSpec(array.shape, lambda n, place: (0,) * array.ndim)
    left_shape = jax.ShapeDtypeStruct((half, left_rows, span), jnp.bfloat16)

    def left_specs(odd):
        mine = lambda n, place: ((place[0] ^ (2 * n + odd)) * CORES + place[1], 0)
        halo = lambda n, place: (place[0] ^ (2 * n + odd), 0)
        return pl.BlockSpec((rows, span), mine), pl.BlockSpec((rows, 6 * PLANE), halo)

    def left_xy(odd, which, vecs, table, place):
        return pl.pallas_call(
            functools.partial(left_xy_kernel, momenta, rows, sites, which),
            grid_spec=pltpu.PrefetchScalarGridSpec(
                num_scalar_prefetch=1,
                grid=(half,),
                in_specs=[left_specs(odd)[0], whole(table), whole(phases)],
                out_specs=pl.BlockSpec((1, 4 * momenta * rows, span), lambda n, place: (n, 0, 0)),
                scratch_shapes=[pltpu.VMEM((18, PLANE), jnp.float32)],
            ),
            out_shape=left_shape,
            compiler_params=params,
            cost_estimate=cost(4e9 if odd == 0 else 1e9),
            name="left_xy",
        )(place, vecs, table, phases)

    def left_z(odd, sides):
        vec_spec, halo_spec = left_specs(odd)
        kept = pl.BlockSpec(memory_space=pl.ANY)
        return pl.pallas_call(
            functools.partial(left_z_kernel, momenta, rows, sites),
            grid_spec=pltpu.PrefetchScalarGridSpec(
                num_scalar_prefetch=1,
                grid=(half,),
                in_specs=[
                    vec_spec, vec_spec, halo_spec, halo_spec, whole(tables), whole(other_tables), whole(phases), kept, kept,
                ],
                out_specs=[pl.BlockSpec((1, 2 * momenta * rows, span), lambda n, place: (n, 2, 0))] * 2,
            ),
            out_shape=[left_shape] * 2,
            input_output_aliases={8: 0, 9: 1},
            compiler_params=params,
            cost_estimate=cost(5e9),
            name="left_z",
        )(place, flat, other, first, second, tables, other_tables, phases, *sides)

    def product(sides, mine, theirs, targets, kinds, first_row=0, size=left_rows, received=()):
        width = sum(piece.shape[0] for piece in mine)
        kept = pl.BlockSpec(memory_space=pl.ANY)
        in_vmem = pl.BlockSpec(memory_space=pltpu.VMEM)
        chunks = [sum(which == n for which, _ in targets) for n in range(len(kinds))]
        return pl.pallas_call(
            functools.partial(product_kernel, sites, half, first_row, size, len(mine), len(received), targets),
            in_specs=[kept] * (2 * len(mine) + 2) + [in_vmem] * len(received),
            out_specs=[in_vmem] * len(kinds),
            out_shape=[jax.ShapeDtypeStruct((n, 2, size, width), kind) for n, kind in zip(chunks, kinds)],
            scratch_shapes=[
                pltpu.VMEM((2 * width, 2 * span), jnp.bfloat16),
                pltpu.VMEM((half * size, 2 * span), jnp.bfloat16),
                pltpu.SemaphoreType.DMA((2, len(mine))),
                pltpu.SemaphoreType.DMA((2, half)),
            ],
            compiler_params=params,
            cost_estimate=cost(7e9 * size / left_rows),
            name="product",
        )(*mine, *theirs, *sides, *received)

    def product_away(sides, right, *rows):
        (away,) = product(sides, *right, [(0, n) for n in range(half)], [jnp.bfloat16], *rows)
        return away, to_chip(away, 1)

    def product_home(sides, right, received):
        if half == 1:
            return product(sides, *right, [(0, 0)], [jnp.float32], received=received)
        targets = [(n % 2, n // 2) for n in range(half)]
        return product(sides, *right, targets, [jnp.float32, jnp.bfloat16], received=received)

    def product_direct(sides, right, odd):
        kinds = [jnp.float32 if n == 0 and not odd else jnp.bfloat16 for n in range(half)]
        outs = product(sides, *right, [(n, 0) for n in range(half)], kinds)
        return outs, [out if 2 * n + odd == 0 else to_chip(out, 2 * n + odd) for n, out in enumerate(outs)]

    scale = 1.0 / math.sqrt(3.0 * sites * slabs)
    spots = 2 * (dirs % 3) + dirs // 3
    out_shape = jax.ShapeDtypeStruct((6, momenta, 2, rows, groups * count), jnp.float32)

    def finish(pieces, places, result):
        at = jnp.concatenate((spots, jnp.stack(places))).astype(jnp.int32)
        in_specs = [pl.BlockSpec((1, 2, left_rows, LANES), lambda n, at: (0, 0, 0, n))] * len(pieces)
        operands = list(pieces)
        aliases = {}
        if result is not None:
            in_specs.append(pl.BlockSpec(memory_space=pl.ANY))
            operands.append(result)
            aliases = {len(operands): 0}
        return pl.pallas_call(
            functools.partial(finish_kernel, len(pieces), momenta, rows, scale),
            grid_spec=pltpu.PrefetchScalarGridSpec(
                num_scalar_prefetch=1,
                grid=(len(places),),
                in_specs=in_specs,
                out_specs=pl.BlockSpec((6, momenta, 2, rows, LANES), lambda n, at: (0, 0, 0, 0, at[6 + n])),
            ),
            out_shape=out_shape,
            input_output_aliases=aliases,
            compiler_params=params,
            cost_estimate=cost(3e9),
            name="finish",
        )(at, *operands)

    def to_chip(array, bit):
        return lax.ppermute(array, "gz", [(i, i ^ (CORES * bit)) for i in range(slabs)])

    def from_group(array, turn):
        return lax.ppermute(array, "vec", [(i, i ^ turn) for i in range(groups)])

    def to_core(arrays):
        return [lax.ppermute(array, "gz", across) for array in arrays]

    def reduce_more(kept, away=None):
        if away is None:
            return [kept]
        pieces, bit = [(kept, 4), (to_chip(away, 2), 4)], 4
        while bit < chips:
            terms = [piece[bit // stride :: 2 * bit // stride].astype(jnp.float32) for piece, stride in pieces]
            away = functools.reduce(jnp.add, terms).astype(jnp.bfloat16)
            pieces.append((to_chip(away, bit), 2 * bit))
            bit *= 2
        return [piece for piece, _ in pieces]

    part = count // 2
    split = groups > 2 and part % LANES == 0
    if split:
        blocks = [[(1, 0), (2, 0)], [(1, 1), (2, 1)]] + [[(turn, None)] for turn in range(3, groups)]
    else:
        blocks = [[(turn, None)] for turn in range(1, groups)]
    source = {None: flat, 0: flat[:part], 1: flat[part:]}
    wide = count // LANES

    def columns(block):
        places = []
        for turn, which in block:
            at = (group ^ turn) * wide
            places += [at + n for n in range(wide)] if which is None else [at + which * (wide // 2) + n for n in range(wide // 2)]
        return places

    def fetch(block, *earlier):
        return [from_group(after(source[which], *earlier) if earlier else source[which], turn) for turn, which in block]

    def own_columns(n):
        return columns([(0, None)] if n == 0 else blocks[n - 1])

    def pass_on(n, earlier):
        mine = [after(array, earlier) for array in arriving[n]]
        mine = [jnp.concatenate(mine, axis=0)] if len(mine) > 1 else mine
        if n < len(blocks):
            arriving[n + 1] = fetch(blocks[n], *mine)
        return mine, to_core(mine)

    def own_columns(n):
        return columns([(0, None)] if n == 0 else blocks[n - 1])

    def pass_on(n, earlier):
        if n not in arriving:
            return
        mine = [after(array, earlier) for array in arriving[n]]
        mine = [jnp.concatenate(mine, axis=0)] if len(mine) > 1 else mine
        if n < len(blocks):
            arriving[n + 1] = fetch(blocks[n], *mine)
        right[n] = (mine, to_core(mine))

    last = len(blocks)
    arriving = {1: fetch(blocks[0])} if blocks else {}
    right = {0: ([flat], [other])}
    flat_rows = 4 * momenta * rows
    sides = {1: [None, None], 0: [None, None]}
    received, sums = {0: []}, {}
    done, result = place, None

    def run(step, n):
        nonlocal done, result
        if step == "left":
            odd, which = n
            vecs, table = ((flat, tables), (other, other_tables))[which]
            sides[odd][which] = done = left_xy(odd, which, vecs, table, after(place, done))
        elif step == "left_z":
            sides[n] = left_z(n, [sides[n][0], after(sides[n][1], done)])
            done = sides[n][0]
        elif step == "pass":
            pass_on(n, done)
        elif step == "finish":
            result = done = finish([after(sums[n][0], done)] + sums[n][1:], own_columns(n), result)
        else:
            even = [after(sides[0][0], done), sides[0][1]]
            odd = [after(sides[1][0], done), sides[1][1]]
            if step == "xy":
                done, arrived = product_away(odd, right[n], 0, flat_rows)
                received[n].append(arrived)
            elif step == "z":
                done, arrived = product_away(odd, right[n], flat_rows, left_rows - flat_rows)
                received[n].append(arrived)
            elif step == "away":
                done, arrived = product_away(odd, right[n], 0, left_rows)
                received[n] = [arrived]
            elif step == "home":
                outs = product_home(even, right[n], received[n])
                sums[n], done = reduce_more(*outs), outs[0]
            elif step == "direct":
                outs, pieces = product_direct(odd if n else even, right[last], n)
                sums[last] = pieces + sums.get(last, []) if n == 0 else sums.get(last, []) + pieces
                done = outs[0]

    for step, n in order(last):
        run(step, n)
    return result


def solution(mesh):
    placed = (P("vec", None, None, "gz"), P(None, None, None, None, "gz"), P(), P())
    return jax.shard_map(
        on_device,
        mesh=mesh,
        in_specs=placed,
        out_specs=P(None, None, None, ("vec", "gz"), None),
        check_vma=False,
    )
```

profile of v0, /device:TPU:17, one launch (start us, length us, event | category | flops | bytes accessed | tf_op | source)
XLA Modules:
  0.0 199.0 jit_solution(10806645618880438527)
XLA Ops:
  0.0 1.0 reshape.7
  1.0 1.9 collective-permute-start.1
  2.9 0.5 collective-permute-start
  3.4 0.7 fusion.1
  4.0 0.1 pad_add_fusion.1.place_ref
  4.1 0.1 pad_add_fusion.4
  4.2 0.7 copy-done
  4.9 0.9 phases.1.phase_ref
  5.8 0.5 copy-done.1
  6.3 1.2 reshape.6.vec_ref.refs_0_.same_ref.cross_ref.own_ref
  7.5 0.0 collective-permute-done
  7.5 0.1 collective-permute-start.4
  7.7 0.1 fusion.2
  7.8 1.3 collective-permute-start.5
  9.1 1.2 collective-permute-start.3
  10.3 4.5 %left_xy.4.refs_2_.refs_0_ = bf16[2,384,3072]{2,1,0:T(8,128)(2,1)} custom-call(s32[2]{0:T(128)S(1)} %pad_add_fusion.1.place_ref, bf16[256,3072]{1,0:T(8,128)(2,1)S(1)} %reshape.6.vec_ref.refs_0_.same_ref.cross_ref.own_ref, f32[4,18,512]{2,1,0:T(8,128)S(1)} %pad_maximum_fusion.link_ref, f32[2,24,512]{2,1,0:T(8,128)S(1)} %phases.1.phase_ref), custom_call_target="tpu_custom_call" | custom-call | flops 1000000000 | bytes 1024 | tf_op jit(solution)/shard_map/left_xy/pallas_call | solution.py:308
  14.8 0.7 edges.1
  15.5 1.8 collective-permute-start.7
  17.3 1.4 collective-permute-start.8
  18.7 0.7 slice_bitcast_fusion
  19.5 0.9 pad_maximum_fusion.1.link_ref.other_link_ref
  20.4 0.0 collective-permute-done.4.vec_ref.refs_1_.other_ref
  20.4 4.5 %left_xy.5.refs_3_.refs_1_ = bf16[2,384,3072]{2,1,0:T(8,128)(2,1)} custom-call(s32[2]{0:T(128)S(1)} %pad_add_fusion.1.place_ref, bf16[256,3072]{1,0:T(8,128)(2,1)S(1)} %collective-permute-done.4.vec_ref.refs_1_.other_ref, f32[4,18,512]{2,1,0:T(8,128)S(1)} %pad_maximum_fusion.1.link_ref.other_link_ref, f32[2,24,512]{2,1,0:T(8,128)S(1)} %phases.1.phase_ref), custom_call_target="tpu_custom_call" | custom-call | flops 1000000000 | bytes 1024 | tf_op jit(solution)/shard_map/left_xy/pallas_call | solution.py:308
  24.9 6.5 %product.9 = bf16[2,2,256,256]{3,2,1,0:T(8,128)(2,1)S(1)} custom-call(bf16[256,3072]{1,0:T(8,128)(2,1)S(1)} %reshape.6.vec_ref.refs_0_.same_ref.cross_ref.own_ref, bf16[256,3072]{1,0:T(8,128)(2,1)S(1)} %collective-permute-done.4.vec_ref.refs_1_.other_ref, bf16[2,384,3072]{2,1,0:T(8,128)(2,1)} %left_xy.4.refs_2_.refs_0_, ...), custom_call_target="tpu_custom_call" | custom-call | flops 4666666496 | bytes 1024 | tf_op jit(solution)/shard_map/product/pallas_call | solution.py:348
  31.4 0.1 constant_dynamic-update-slice_fusion.1
  31.5 0.1 constant_dynamic-update-slice_fusion.refs_0_
  31.5 0.3 collective-permute-start.9
  31.8 0.3 collective-permute-start.6
  32.1 0.2 collective-permute-start.11
  32.3 4.4 %collective-permute-done.8.second_ref = bf16[128,1536]{1,0:T(8,128)(2,1)S(1)} collective-permute-done((bf16[128,1536]{1,0:T(8,128)(2,1)S(1)}, bf16[128,1536]{1,0:T(8,128)(2,1)S(1)}, u32[]{:S(2)}, u32[]{:S(2)}) %collective-permute-start.8) | collective-permute-done | bytes 393248 | tf_op jit(solution)/shard_map/ppermute | solution.py:285
  36.7 3.8 %left_z.2 = (bf16[2,384,3072]{2,1,0:T(8,128)(2,1)}, bf16[2,384,3072]{2,1,0:T(8,128)(2,1)}) custom-call(s32[2]{0:T(128)S(1)} %pad_add_fusion.1.place_ref, bf16[256,3072]{1,0:T(8,128)(2,1)S(1)} %reshape.6.vec_ref.refs_0_.same_ref.cross_ref.own_ref, ...), custom_call_target="tpu_custom_call", output_to_operand_aliasing={{0}: (8, {}), {1}: (9, {})} | custom-call | flops 5000000000 | bytes 1024 | tf_op jit(solution)/shard_map/left_z/pallas_call | solution.py:326
  40.5 3.9 %product.10 = bf16[2,2,128,256]{3,2,1,0:T(8,128)(2,1)S(1)} custom-call(bf16[256,3072]{1,0:T(8,128)(2,1)S(1)} %reshape.6.vec_ref.refs_0_.same_ref.cross_ref.own_ref, bf16[256,3072]{1,0:T(8,128)(2,1)S(1)} %collective-permute-done.4.vec_ref.refs_1_.other_ref, bf16[2,384,3072]{2,1,0:T(8,128)(2,1)} %get-tuple-element.78.refs_2_, ...), custom_call_target="tpu_custom_call" | custom-call | flops 2333333248 | bytes 1024 | tf_op jit(solution)/shard_map/product/pallas_call | solution.py:348
  44.4 1.1 collective-permute-start.13
  45.5 0.5 collective-permute-start.12
  45.9 4.6 %left_xy.6.refs_0_ = bf16[2,384,3072]{2,1,0:T(8,128)(2,1)} custom-call(s32[2]{0:T(128)S(1)} %pad_add_fusion.1.place_ref, bf16[256,3072]{1,0:T(8,128)(2,1)S(1)} %reshape.6.vec_ref.refs_0_.same_ref.cross_ref.own_ref, f32[4,18,512]{2,1,0:T(8,128)S(1)} %pad_maximum_fusion.link_ref, f32[2,24,512]{2,1,0:T(8,128)S(1)} %phases.1.phase_ref), custom_call_target="tpu_custom_call" | custom-call | flops 4000000000 | bytes 1024 | tf_op jit(solution)/shard_map/left_xy/pallas_call | solution.py:308
  50.5 4.6 %left_xy.7.refs_1_ = bf16[2,384,3072]{2,1,0:T(8,128)(2,1)} custom-call(s32[2]{0:T(128)S(1)} %pad_add_fusion.1.place_ref, bf16[256,3072]{1,0:T(8,128)(2,1)S(1)} %collective-permute-done.4.vec_ref.refs_1_.other_ref, f32[4,18,512]{2,1,0:T(8,128)S(1)} %pad_maximum_fusion.1.link_ref.other_link_ref, f32[2,24,512]{2,1,0:T(8,128)S(1)} %phases.1.phase_ref), custom_call_target="tpu_custom_call" | custom-call | flops 4000000000 | bytes 1024 | tf_op jit(solution)/shard_map/left_xy/pallas_call | solution.py:308
  55.1 0.1 constant_dynamic-update-slice_fusion.3
  55.1 0.1 constant_dynamic-update-slice_fusion.2.refs_0_
  55.2 0.1 collective-permute-start.15
  55.3 0.3 collective-permute-start.10
  55.5 3.8 %left_z.3 = (bf16[2,384,3072]{2,1,0:T(8,128)(2,1)}, bf16[2,384,3072]{2,1,0:T(8,128)(2,1)}) custom-call(s32[2]{0:T(128)S(1)} %pad_add_fusion.1.place_ref, bf16[256,3072]{1,0:T(8,128)(2,1)S(1)} %reshape.6.vec_ref.refs_0_.same_ref.cross_ref.own_ref, ...), custom_call_target="tpu_custom_call", output_to_operand_aliasing={{0}: (8, {}), {1}: (9, {})} | custom-call | flops 5000000000 | bytes 1024 | tf_op jit(solution)/shard_map/left_z/pallas_call | solution.py:326
  59.3 9.1 %product.11 = bf16[2,2,384,256]{3,2,1,0:T(8,128)(2,1)S(1)} custom-call(bf16[256,3072]{1,0:T(8,128)(2,1)S(1)} %constant_dynamic-update-slice_fusion.refs_0_, bf16[256,3072]{1,0:T(8,128)(2,1)S(1)} %collective-permute-done.11.refs_1_, bf16[2,384,3072]{2,1,0:T(8,128)(2,1)} %get-tuple-element.78.refs_2_, bf16[2,384,3072]{2,1,0:T(8,128)(2,1)} %get-tuple-element.60.refs_3_), custom_call_target="tpu_custom_call" | custom-call | flops 7000000000 | bytes 1024 | tf_op jit(solution)/shard_map/product/pallas_call | solution.py:348
  68.4 1.1 collective-permute-start.16
  69.4 9.0 %product.12 = (f32[1,2,384,256]{3,2,1,0:T(8,128)S(1)}, bf16[1,2,384,256]{3,2,1,0:T(8,128)(2,1)S(1)}) custom-call(bf16[256,3072]{1,0:T(8,128)(2,1)S(1)} %reshape.6.vec_ref.refs_0_.same_ref.cross_ref.own_ref, bf16[256,3072]{1,0:T(8,128)(2,1)S(1)} %collective-permute-done.4.vec_ref.refs_1_.other_ref, bf16[2,384,3072]{2,1,0:T(8,128)(2,1)} %get-tuple-element.82.refs_2_, ...), custom_call_target="tpu_custom_call" | custom-call | flops 7000000000 | bytes 1024 | tf_op jit(solution)/shard_map/product/pallas_call | solution.py:348
  78.5 1.7 collective-permute-start.17
  80.2 11.6 %collective-permute-done.10.refs_0_ = bf16[256,3072]{1,0:T(8,128)(2,1)S(1)} collective-permute-done((bf16[256,3072]{1,0:T(8,128)(2,1)S(1)}, bf16[256,3072]{1,0:T(8,128)(2,1)S(1)}, u32[]{:S(2)}, u32[]{:S(2)}) %collective-permute-start.10) | collective-permute-done | bytes 1572896 | tf_op jit(solution)/shard_map/ppermute | solution.py:411
  91.8 1.3 collective-permute-start.14
  93.0 9.0 %product.13 = bf16[2,2,384,256]{3,2,1,0:T(8,128)(2,1)S(1)} custom-call(bf16[256,3072]{1,0:T(8,128)(2,1)S(1)} %constant_dynamic-update-slice_fusion.2.refs_0_, bf16[256,3072]{1,0:T(8,128)(2,1)S(1)} %collective-permute-done.15.refs_1_, bf16[2,384,3072]{2,1,0:T(8,128)(2,1)} %get-tuple-element.78.refs_2_, bf16[2,384,3072]{2,1,0:T(8,128)(2,1)} %get-tuple-element.60.refs_3_), custom_call_target="tpu_custom_call" | custom-call | flops 7000000000 | bytes 1024 | tf_op jit(solution)/shard_map/product/pallas_call | solution.py:348
  102.1 1.1 collective-permute-start.18
  103.2 9.1 %product.14 = (f32[1,2,384,256]{3,2,1,0:T(8,128)S(1)}, bf16[1,2,384,256]{3,2,1,0:T(8,128)(2,1)S(1)}) custom-call(bf16[256,3072]{1,0:T(8,128)(2,1)S(1)} %constant_dynamic-update-slice_fusion.refs_0_, bf16[256,3072]{1,0:T(8,128)(2,1)S(1)} %collective-permute-done.11.refs_1_, bf16[2,384,3072]{2,1,0:T(8,128)(2,1)} %get-tuple-element.82.refs_2_, ...), custom_call_target="tpu_custom_call" | custom-call | flops 7000000000 | bytes 1024 | tf_op jit(solution)/shard_map/product/pallas_call | solution.py:348
  112.3 1.6 finish.4.refs_2_
  113.9 1.7 collective-permute-start.19
  115.6 9.0 %product.15 = (bf16[1,2,384,256]{3,2,1,0:T(8,128)(2,1)S(1)}, bf16[1,2,384,256]{3,2,1,0:T(8,128)(2,1)S(1)}) custom-call(bf16[256,3072]{1,0:T(8,128)(2,1)S(1)} %collective-permute-done.10.refs_0_, bf16[256,3072]{1,0:T(8,128)(2,1)S(1)} %collective-permute-done.14.refs_1_, bf16[2,384,3072]{2,1,0:T(8,128)(2,1)} %get-tuple-element.78.refs_2_, ...), custom_call_target="tpu_custom_call" | custom-call | flops 7000000000 | bytes 1024 | tf_op jit(solution)/shard_map/product/pallas_call | solution.py:348
  124.6 9.0 %product.16 = (f32[1,2,384,256]{3,2,1,0:T(8,128)S(1)}, bf16[1,2,384,256]{3,2,1,0:T(8,128)(2,1)S(1)}) custom-call(bf16[256,3072]{1,0:T(8,128)(2,1)S(1)} %collective-permute-done.10.refs_0_, bf16[256,3072]{1,0:T(8,128)(2,1)S(1)} %collective-permute-done.14.refs_1_, bf16[2,384,3072]{2,1,0:T(8,128)(2,1)} %get-tuple-element.82.refs_2_, ...), custom_call_target="tpu_custom_call" | custom-call | flops 7000000000 | bytes 1024 | tf_op jit(solution)/shard_map/product/pallas_call | solution.py:348
  133.7 9.1 %product.17 = (f32[1,2,384,256]{3,2,1,0:T(8,128)S(1)}, bf16[1,2,384,256]{3,2,1,0:T(8,128)(2,1)S(1)}) custom-call(bf16[256,3072]{1,0:T(8,128)(2,1)S(1)} %constant_dynamic-update-slice_fusion.2.refs_0_, bf16[256,3072]{1,0:T(8,128)(2,1)S(1)} %collective-permute-done.15.refs_1_, bf16[2,384,3072]{2,1,0:T(8,128)(2,1)} %get-tuple-element.82.refs_2_, ...), custom_call_target="tpu_custom_call" | custom-call | flops 7000000000 | bytes 1024 | tf_op jit(solution)/shard_map/product/pallas_call | solution.py:348
  142.8 0.8 collective-permute-start.20
  143.5 0.8 collective-permute-start.22
  144.4 2.3 %collective-permute-start.21 = (bf16[1,2,384,256]{3,2,1,0:T(8,128)(2,1)S(1)}, bf16[1,2,384,256]{3,2,1,0:T(8,128)(2,1)S(1)}, u32[]{:S(2)}, u32[]{:S(2)}) collective-permute-start(bf16[1,2,384,256]{3,2,1,0:T(8,128)(2,1)S(1)} %get-tuple-element.89), channel_id=1, source_target_pairs={{0,4},{1,5},{2,6},{3,7},{4,0},{5,1},{6,2},{7,3},{8,12},{9,13},{10,... | collective-permute-start | bytes 1179656 | tf_op jit(solution)/shard_map/ppermute | solution.py:408
  146.7 1.6 finish.5.refs_2_
  148.3 12.1 %collective-permute-done.20.refs_1_ = bf16[1,2,384,256]{3,2,1,0:T(8,128)(2,1)S(1)} collective-permute-done((bf16[1,2,384,256]{3,2,1,0:T(8,128)(2,1)S(1)}, bf16[1,2,384,256]{3,2,1,0:T(8,128)(2,1)S(1)}, u32[]{:S(2)}, u32[]{:S(2)}) %collective-permute-start.20) | collective-permute-done | bytes 393248 | tf_op jit(solution)/shard_map/ppermute | solution.py:408
  160.4 1.6 finish.6.refs_4_
  162.0 23.7 %collective-permute-done.21.refs_1_ = bf16[1,2,384,256]{3,2,1,0:T(8,128)(2,1)S(1)} collective-permute-done((bf16[1,2,384,256]{3,2,1,0:T(8,128)(2,1)S(1)}, bf16[1,2,384,256]{3,2,1,0:T(8,128)(2,1)S(1)}, u32[]{:S(2)}, u32[]{:S(2)}) %collective-permute-start.21) | collective-permute-done | bytes 393248 | tf_op jit(solution)/shard_map/ppermute | solution.py:408
  185.6 11.3 %collective-permute-done.23.refs_3_ = bf16[1,2,384,256]{3,2,1,0:T(8,128)(2,1)S(1)} collective-permute-done((bf16[1,2,384,256]{3,2,1,0:T(8,128)(2,1)S(1)}, bf16[1,2,384,256]{3,2,1,0:T(8,128)(2,1)S(1)}, u32[]{:S(2)}, u32[]{:S(2)}) %collective-permute-start.23) | collective-permute-done | bytes 393248 | tf_op jit(solution)/shard_map/ppermute | solution.py:408
  196.9 1.8 finish.7
  (26 shorter events, 0.1 us)
Async XLA Ops:
  1.0 6.5 %collective-permute-start.1 = (f32[18,256]{1,0:T(8,128)S(1)}, f32[18,256]{1,0:T(8,128)S(1)}, u32[]{:S(2)}, u32[]{:S(2)}) collective-permute-start(f32[18,256]{1,0:T(8,128)S(1)} %get-tuple-element.94), channel_id=1, source_target_pairs={{0,1},{1,2},{2,3},{3,4},{4,5},{5,6},{6,7},{7,0},{8,9},{9,10},{10,1... | collective-permute-start | bytes 55304 | tf_op jit(solution)/shard_map/ppermute | solution.py:253
  2.9 4.6 %collective-permute-start.2 = (f32[18,256]{1,0:T(8,128)S(1)}, f32[18,256]{1,0:T(8,128)S(1)}, u32[]{:S(2)}, u32[]{:S(2)}) collective-permute-start(f32[18,256]{1,0:T(8,128)S(1)} %get-tuple-element.94), channel_id=1, source_target_pairs={{0,2},{1,3},{2,4},{3,5},{4,6},{5,7},{6,0},{7,1},{8,10},{9,11},{10,... | collective-permute-start | bytes 55304 | tf_op jit(solution)/shard_map/ppermute | solution.py:254
  2.9 4.6 %collective-permute-start = (f32[3,18,512]{2,1,0:T(8,128)S(1)}, f32[3,18,512]{2,1,0:T(8,128)}, u32[]{:S(2)}, u32[]{:S(2)}) collective-permute-start(f32[3,18,512]{2,1,0:T(8,128)S(1)} %reshape.7), channel_id=1, source_target_pairs={{0,1},{1,0},{2,3},{3,2},{4,5},{5,4},{6,7},{7,6},{8,9},{9,8},{10,11... | collective-permute-start | bytes 331784 | tf_op jit(solution)/shard_map/ppermute | solution.py:252
  4.2 0.7 copy-start
  4.9 1.4 copy-start.1
  7.5 12.9 %collective-permute-start.4 = (bf16[256,3072]{1,0:T(8,128)(2,1)S(1)}, bf16[256,3072]{1,0:T(8,128)(2,1)S(1)}, u32[]{:S(2)}, u32[]{:S(2)}) collective-permute-start(bf16[256,3072]{1,0:T(8,128)(2,1)S(1)} %reshape.6.vec_ref.refs_0_.same_ref.cross_ref.own_ref), channel_id=1, source_target_pairs={{0,1},{1,0},{2,3},{3,2},{4,5},{5,4},{6,7},{7,6},{8,9},{9,8},{10,11... | collective-permute-start | bytes 4718600 | tf_op jit(solution)/shard_map/ppermute | solution.py:264
  7.8 23.7 %collective-permute-start.5 = (bf16[128,3072]{1,0:T(8,128)(2,1)S(1)}, bf16[128,3072]{1,0:T(8,128)(2,1)S(1)}, u32[]{:S(2)}, u32[]{:S(2)}) collective-permute-start(bf16[128,3072]{1,0:T(8,128)(2,1)S(1)} %get-tuple-element.91), channel_id=1, source_target_pairs={{0,16},{8,24},{16,0},{24,8},{1,17},{9,25},{17,1},{25,9},{2,18},{10... | collective-permute-start | bytes 2359304 | tf_op jit(solution)/shard_map/ppermute | solution.py:411
  9.1 22.3 %collective-permute-start.3 = (bf16[128,3072]{1,0:T(8,128)(2,1)S(1)}, bf16[128,3072]{1,0:T(8,128)(2,1)S(1)}, u32[]{:S(2)}, u32[]{:S(2)}) collective-permute-start(bf16[128,3072]{1,0:T(8,128)(2,1)S(1)} %get-tuple-element.91), channel_id=1, source_target_pairs={{0,8},{8,0},{16,24},{24,16},{1,9},{9,1},{17,25},{25,17},{2,10},{10... | collective-permute-start | bytes 2359304 | tf_op jit(solution)/shard_map/ppermute | solution.py:411
  15.5 16.8 %collective-permute-start.7 = (bf16[128,1536]{1,0:T(8,128)(2,1)S(1)}, bf16[128,1536]{1,0:T(8,128)(2,1)S(1)}, u32[]{:S(2)}, u32[]{:S(2)}) collective-permute-start(bf16[128,1536]{1,0:T(8,128)(2,1)S(1)} %get-tuple-element.55), channel_id=1, source_target_pairs={{0,6},{1,3},{2,0},{3,5},{4,2},{5,7},{6,4},{7,1},{8,14},{9,11},{10,... | collective-permute-start | bytes 1179656 | tf_op jit(solution)/shard_map/ppermute | solution.py:284
  17.3 19.4 %collective-permute-start.8 = (bf16[128,1536]{1,0:T(8,128)(2,1)S(1)}, bf16[128,1536]{1,0:T(8,128)(2,1)S(1)}, u32[]{:S(2)}, u32[]{:S(2)}) collective-permute-start(bf16[128,1536]{1,0:T(8,128)(2,1)S(1)} %get-tuple-element.56), channel_id=1, source_target_pairs={{0,7},{1,2},{2,1},{3,4},{4,3},{5,6},{6,5},{7,0},{8,15},{9,10},{10,... | collective-permute-start | bytes 1179656 | tf_op jit(solution)/shard_map/ppermute | solution.py:285
  31.5 23.5 %collective-permute-start.9 = (bf16[128,3072]{1,0:T(8,128)(2,1)S(1)}, bf16[128,3072]{1,0:T(8,128)(2,1)S(1)}, u32[]{:S(2)}, u32[]{:S(2)}) collective-permute-start(bf16[128,3072]{1,0:T(8,128)(2,1)S(1)} %get-tuple-element.54), channel_id=1, source_target_pairs={{0,16},{8,24},{16,0},{24,8},{1,17},{9,25},{17,1},{25,9},{2,18},{10... | collective-permute-start | bytes 2359304 | tf_op jit(solution)/shard_map/ppermute | solution.py:411
  31.8 23.2 %collective-permute-start.6 = (bf16[128,3072]{1,0:T(8,128)(2,1)S(1)}, bf16[128,3072]{1,0:T(8,128)(2,1)S(1)}, u32[]{:S(2)}, u32[]{:S(2)}) collective-permute-start(bf16[128,3072]{1,0:T(8,128)(2,1)S(1)} %get-tuple-element.54), channel_id=1, source_target_pairs={{0,8},{8,0},{16,24},{24,16},{1,9},{9,1},{17,25},{25,17},{2,10},{10... | collective-permute-start | bytes 2359304 | tf_op jit(solution)/shard_map/ppermute | solution.py:411
  32.1 27.2 %collective-permute-start.11 = (bf16[256,3072]{1,0:T(8,128)(2,1)S(1)}, bf16[256,3072]{1,0:T(8,128)(2,1)S(1)}, u32[]{:S(2)}, u32[]{:S(2)}) collective-permute-start(bf16[256,3072]{1,0:T(8,128)(2,1)S(1)} %constant_dynamic-update-slice_fusion.refs_0_), channel_id=1, source_target_pairs={{0,1},{1,0},{2,3},{3,2},{4,5},{5,4},{6,7},{7,6},{8,9},{9,8},{10,11... | collective-permute-start | bytes 4718600 | tf_op jit(solution)/shard_map/ppermute | solution.py:414
  44.4 25.0 %collective-permute-start.13 = (bf16[2,2,128,256]{3,2,1,0:T(8,128)(2,1)S(1)}, bf16[2,2,128,256]{3,2,1,0:T(8,128)(2,1)S(1)}, u32[]{:S(2)}, u32[]{:S(2)}) collective-permute-start(bf16[2,2,128,256]{3,2,1,0:T(8,128)(2,1)S(1)} %product.10), channel_id=1, source_target_pairs={{0,2},{1,3},{2,0},{3,1},{4,6},{5,7},{6,4},{7,5},{8,10},{9,11},{10,... | collective-permute-start | bytes 786440 | tf_op jit(solution)/shard_map/ppermute | solution.py:408
  45.5 24.0 %collective-permute-start.12 = (bf16[2,2,256,256]{3,2,1,0:T(8,128)(2,1)S(1)}, bf16[2,2,256,256]{3,2,1,0:T(8,128)(2,1)S(1)}, u32[]{:S(2)}, u32[]{:S(2)}) collective-permute-start(bf16[2,2,256,256]{3,2,1,0:T(8,128)(2,1)S(1)} %product.9), channel_id=1, source_target_pairs={{0,2},{1,3},{2,0},{3,1},{4,6},{5,7},{6,4},{7,5},{8,10},{9,11},{10,... | collective-permute-start | bytes 1572872 | tf_op jit(solution)/shard_map/ppermute | solution.py:408
  55.2 37.9 %collective-permute-start.15 = (bf16[256,3072]{1,0:T(8,128)(2,1)S(1)}, bf16[256,3072]{1,0:T(8,128)(2,1)S(1)}, u32[]{:S(2)}, u32[]{:S(2)}) collective-permute-start(bf16[256,3072]{1,0:T(8,128)(2,1)S(1)} %constant_dynamic-update-slice_fusion.2.refs_0_), channel_id=1, source_target_pairs={{0,1},{1,0},{2,3},{3,2},{4,5},{5,4},{6,7},{7,6},{8,9},{9,8},{10,11... | collective-permute-start | bytes 4718600 | tf_op jit(solution)/shard_map/ppermute | solution.py:414
  55.3 36.5 %collective-permute-start.10 = (bf16[256,3072]{1,0:T(8,128)(2,1)S(1)}, bf16[256,3072]{1,0:T(8,128)(2,1)S(1)}, u32[]{:S(2)}, u32[]{:S(2)}) collective-permute-start(bf16[256,3072]{1,0:T(8,128)(2,1)S(1)} %reshape.6.vec_ref.refs_0_.same_ref.cross_ref.own_ref), channel_id=1, source_target_pairs={{0,24},{8,16},{16,8},{24,0},{1,25},{9,17},{17,9},{25,1},{2,26},{10... | collective-permute-start | bytes 4718600 | tf_op jit(solution)/shard_map/ppermute | solution.py:411
  68.4 34.8 %collective-permute-start.16 = (bf16[2,2,384,256]{3,2,1,0:T(8,128)(2,1)S(1)}, bf16[2,2,384,256]{3,2,1,0:T(8,128)(2,1)S(1)}, u32[]{:S(2)}, u32[]{:S(2)}) collective-permute-start(bf16[2,2,384,256]{3,2,1,0:T(8,128)(2,1)S(1)} %product.11), channel_id=1, source_target_pairs={{0,2},{1,3},{2,0},{3,1},{4,6},{5,7},{6,4},{7,5},{8,10},{9,11},{10,... | collective-permute-start | bytes 2359304 | tf_op jit(solution)/shard_map/ppermute | solution.py:408
  78.5 33.8 %collective-permute-start.17 = (bf16[1,2,384,256]{3,2,1,0:T(8,128)(2,1)S(1)}, bf16[1,2,384,256]{3,2,1,0:T(8,128)(2,1)S(1)}, u32[]{:S(2)}, u32[]{:S(2)}) collective-permute-start(bf16[1,2,384,256]{3,2,1,0:T(8,128)(2,1)S(1)} %get-tuple-element.77), channel_id=1, source_target_pairs={{0,4},{1,5},{2,6},{3,7},{4,0},{5,1},{6,2},{7,3},{8,12},{9,13},{10,... | collective-permute-start | bytes 1179656 | tf_op jit(solution)/shard_map/ppermute | solution.py:408
  91.8 23.8 %collective-permute-start.14 = (bf16[256,3072]{1,0:T(8,128)(2,1)S(1)}, bf16[256,3072]{1,0:T(8,128)(2,1)S(1)}, u32[]{:S(2)}, u32[]{:S(2)}) collective-permute-start(bf16[256,3072]{1,0:T(8,128)(2,1)S(1)} %collective-permute-done.10.refs_0_), channel_id=1, source_target_pairs={{0,1},{1,0},{2,3},{3,2},{4,5},{5,4},{6,7},{7,6},{8,9},{9,8},{10,11... | collective-permute-start | bytes 4718600 | tf_op jit(solution)/shard_map/ppermute | solution.py:414
  102.1 31.6 %collective-permute-start.18 = (bf16[2,2,384,256]{3,2,1,0:T(8,128)(2,1)S(1)}, bf16[2,2,384,256]{3,2,1,0:T(8,128)(2,1)S(1)}, u32[]{:S(2)}, u32[]{:S(2)}) collective-permute-start(bf16[2,2,384,256]{3,2,1,0:T(8,128)(2,1)S(1)} %product.13), channel_id=1, source_target_pairs={{0,2},{1,3},{2,0},{3,1},{4,6},{5,7},{6,4},{7,5},{8,10},{9,11},{10,... | collective-permute-start | bytes 2359304 | tf_op jit(solution)/shard_map/ppermute | solution.py:408
  113.9 32.8 %collective-permute-start.19 = (bf16[1,2,384,256]{3,2,1,0:T(8,128)(2,1)S(1)}, bf16[1,2,384,256]{3,2,1,0:T(8,128)(2,1)S(1)}, u32[]{:S(2)}, u32[]{:S(2)}) collective-permute-start(bf16[1,2,384,256]{3,2,1,0:T(8,128)(2,1)S(1)} %get-tuple-element.85), channel_id=1, source_target_pairs={{0,4},{1,5},{2,6},{3,7},{4,0},{5,1},{6,2},{7,3},{8,12},{9,13},{10,... | collective-permute-start | bytes 1179656 | tf_op jit(solution)/shard_map/ppermute | solution.py:408
  142.8 17.6 %collective-permute-start.20 = (bf16[1,2,384,256]{3,2,1,0:T(8,128)(2,1)S(1)}, bf16[1,2,384,256]{3,2,1,0:T(8,128)(2,1)S(1)}, u32[]{:S(2)}, u32[]{:S(2)}) collective-permute-start(bf16[1,2,384,256]{3,2,1,0:T(8,128)(2,1)S(1)} %get-tuple-element.87), channel_id=1, source_target_pairs={{0,4},{1,5},{2,6},{3,7},{4,0},{5,1},{6,2},{7,3},{8,12},{9,13},{10,... | collective-permute-start | bytes 1179656 | tf_op jit(solution)/shard_map/ppermute | solution.py:408
  143.5 42.1 %collective-permute-start.22 = (bf16[1,2,384,256]{3,2,1,0:T(8,128)(2,1)S(1)}, bf16[1,2,384,256]{3,2,1,0:T(8,128)(2,1)S(1)}, u32[]{:S(2)}, u32[]{:S(2)}) collective-permute-start(bf16[1,2,384,256]{3,2,1,0:T(8,128)(2,1)S(1)} %get-tuple-element.79), channel_id=1, source_target_pairs={{0,2},{1,3},{2,0},{3,1},{4,6},{5,7},{6,4},{7,5},{8,10},{9,11},{10,... | collective-permute-start | bytes 1179656 | tf_op jit(solution)/shard_map/ppermute | solution.py:408
  144.4 41.3 %collective-permute-start.21 = (bf16[1,2,384,256]{3,2,1,0:T(8,128)(2,1)S(1)}, bf16[1,2,384,256]{3,2,1,0:T(8,128)(2,1)S(1)}, u32[]{:S(2)}, u32[]{:S(2)}) collective-permute-start(bf16[1,2,384,256]{3,2,1,0:T(8,128)(2,1)S(1)} %get-tuple-element.89), channel_id=1, source_target_pairs={{0,4},{1,5},{2,6},{3,7},{4,0},{5,1},{6,2},{7,3},{8,12},{9,13},{10,... | collective-permute-start | bytes 1179656 | tf_op jit(solution)/shard_map/ppermute | solution.py:408
  146.7 50.2 %collective-permute-start.23 = (bf16[1,2,384,256]{3,2,1,0:T(8,128)(2,1)S(1)}, bf16[1,2,384,256]{3,2,1,0:T(8,128)(2,1)S(1)}, u32[]{:S(2)}, u32[]{:S(2)}) collective-permute-start(bf16[1,2,384,256]{3,2,1,0:T(8,128)(2,1)S(1)} %get-tuple-element.90), channel_id=1, source_target_pairs={{0,6},{1,7},{2,4},{3,5},{4,2},{5,3},{6,0},{7,1},{8,14},{9,15},{10,... | collective-permute-start | bytes 1179656 | tf_op jit(solution)/shard_map/ppermute | solution.py:408
where the time goes:
time: 202 us; the launch traced here: 199 us
  Pallas kernels  108 us (53%)
  waiting for transfers between devices  62.9 us (31%)
  starting transfers between devices  21.6 us (11%)
  local copies, waits for them, and re-layouts  4.34 us (2%)
    pallas_call x9, Pallas kernels, product(): pl.pallas_call(functools.partial(product_kernel, sites, half, first_row,...  73.8 us
    ppermute x10, waiting for transfers between devices, to_chip(): lax.ppermute(array, 'gz', [(i, i ^ CORES * bit) for i in range(slabs)])  47 us
    pallas_call x4, Pallas kernels, left_xy(): pl.pallas_call(functools.partial(left_xy_kernel, momenta, rows, sites, wh...  18.1 us
    ppermute x5, waiting for transfers between devices, from_group(): return lax.ppermute(array, 'vec', [(i, i ^ turn) for i in range(groups)])  11.6 us
    ppermute x10, starting transfers between devices, to_chip(): lax.ppermute(array, 'gz', [(i, i ^ CORES * bit) for i in range(slabs)])  11 us
    pallas_call x2, Pallas kernels, left_z(): pl.pallas_call(functools.partial(left_z_kernel, momenta, rows, sites), gr...  7.55 us
    pallas_call x4, Pallas kernels, finish(): pl.pallas_call(functools.partial(finish_kernel, len(pieces), momenta, row...  6.68 us
    ppermute x1, waiting for transfers between devices, on_device(): second = lax.ppermute(cross, 'gz', [(i, step(i) ^ 1) for i in range(slabs)])  4.36 us
  transfers between devices with their start and end apart: 24, of which 5 were waited for; matrix products, arithmetic and copies ran while one was open for 2% of the time, Pallas kernels for 53%

commit v1 on v0

--- a/solution.py
+++ b/solution.py
@@ -15,6 +15,7 @@
 CORES = 2
 VMEM_BYTES = 48 * 1024 * 1024
 COST_SCALE = 1.0
+ROWS = 384
 
 
 def cost(work):
@@ -80,12 +81,11 @@
     out_ref[1] = jnp.sin(angles[...])
 
 
-def edge_kernel(sites, place_ref, same_ref, cross_ref, same_out, cross_out):
-    for ref, out in ((same_ref, same_out), (cross_ref, cross_out)):
-        for c in range(6):
-            lowest = ref[:, pl.ds(c * sites, PLANE)]
-            highest = ref[:, pl.ds((c + 1) * sites - PLANE, PLANE)]
-            out[:, pl.ds(c * PLANE, PLANE)] = jnp.where(place_ref[1] == 0, lowest, highest)
+def edge_kernel(sites, place_ref, vec_ref, out_ref):
+    for c in range(6):
+        lowest = vec_ref[:, pl.ds(c * sites, PLANE)]
+        highest = vec_ref[:, pl.ds((c + 1) * sites - PLANE, PLANE)]
+        out_ref[:, pl.ds(c * PLANE, PLANE)] = jnp.where(place_ref[1] == 0, lowest, highest)
 
 
 def left_xy_kernel(momenta, rows, sites, slab, place_ref, vec_ref, link_ref, phase_ref, out_ref, table):
@@ -144,58 +144,68 @@
                 store_left(refs[2 + slab], 0, slab, 2, sign_at, at, moved, link, phase_ref, momenta, rows, sites)
 
 
-def product_kernel(sites, half, first_row, size, parts, received, targets, *refs):
+def product_kernel(sites, half, first_row, size, parts, pairs, received, targets, *refs):
     mine, theirs = refs[:parts], refs[parts : 2 * parts]
-    left = refs[2 * parts : 2 * parts + 2]
-    got = refs[2 * parts + 2 : 2 * parts + 2 + received]
-    *outs, right, rows, right_sems, left_sems = refs[2 * parts + 2 + received :]
+    left = refs[2 * parts : 2 * parts + 2 * pairs]
+    got = refs[2 * parts + 2 * pairs : 2 * parts + 2 * pairs + received]
+    *outs, right, rows, right_sems, left_sems = refs[2 * parts + 2 * pairs + received :]
     width = right.shape[0] // 2
     span = 6 * sites
+    chunks = half * pairs
     columns = [pl.ds(slab * span, span) for slab in range(2)]
-    copies = [[], []]
+    right_copies, left_copies = [[], []], [[], []]
     for slab, pieces in enumerate((mine, theirs)):
         start = 0
         for n, piece in enumerate(pieces):
             count = piece.shape[0]
-            copies[slab].append(
+            right_copies[slab].append(
                 pltpu.make_async_copy(piece, right.at[pl.ds(start, count), columns[slab]], right_sems.at[slab, n])
             )
             start += count
-        for n in range(half):
-            copies[slab].append(
+        for n in range(chunks):
+            left_copies[slab].append(
                 pltpu.make_async_copy(
-                    left[slab].at[n, pl.ds(first_row, size)], rows.at[pl.ds(n * size, size), columns[slab]],
-                    left_sems.at[slab, n],
+                    left[2 * (n // half) + slab].at[n % half, pl.ds(first_row, size)],
+                    rows.at[pl.ds(n * size, size), columns[slab]], left_sems.at[slab, n],
                 )
             )
-    for slab in range(2):
-        for copy in copies[slab]:
-            copy.start()
-    sums = None
-    for slab in range(2):
-        for copy in copies[slab]:
-            copy.wait()
-        for colour in range(3):
-            real_at = slab * span + 2 * colour * sites
-            imag_at = real_at + sites
-            right[pl.ds(width, width), pl.ds(real_at, sites)] = right[pl.ds(0, width), pl.ds(imag_at, sites)]
-            right[pl.ds(width, width), pl.ds(imag_at, sites)] = -right[pl.ds(0, width), pl.ds(real_at, sites)]
-        part = lax.dot_general(
-            rows[:, columns[slab]], right[:, columns[slab]], (((1,), (1,)), ((), ())),
-            preferred_element_type=jnp.float32,
-        )
-        sums = part if sums is None else sums + part
-    for n, (which, place) in enumerate(targets):
-        for q in range(2):
-            total = sums[n * size : (n + 1) * size, q * width : (q + 1) * width]
-            if not got:
-                outs[which][place, q] = total.astype(outs[which].dtype)
-            start = 0
-            for ref in got:
-                count = ref.shape[2]
-                added = total[start : start + count] + ref[n, q].astype(jnp.float32)
-                outs[which][place, q, pl.ds(start, count)] = added.astype(outs[which].dtype)
-                start += count
+    together = max(1, ROWS // size)
+    groups = [range(n, min(n + together, chunks)) for n in range(0, chunks, together)]
+    for group in groups:
+        for slab in range(2):
+            for copy in (right_copies[slab] if group is groups[0] else []) + [left_copies[slab][n] for n in group]:
+                copy.start()
+    for group in groups:
+        sums = None
+        here = pl.ds(group[0] * size, len(group) * size)
+        for slab in range(2):
+            if group is groups[0]:
+                for copy in right_copies[slab]:
+                    copy.wait()
+                for colour in range(3):
+                    real_at = slab * span + 2 * colour * sites
+                    imag_at = real_at + sites
+                    right[pl.ds(width, width), pl.ds(real_at, sites)] = right[pl.ds(0, width), pl.ds(imag_at, sites)]
+                    right[pl.ds(width, width), pl.ds(imag_at, sites)] = -right[pl.ds(0, width), pl.ds(real_at, sites)]
+            for n in group:
+                left_copies[slab][n].wait()
+            part = lax.dot_general(
+                rows[here, columns[slab]], right[:, columns[slab]], (((1,), (1,)), ((), ())),
+                preferred_element_type=jnp.float32,
+            )
+            sums = part if sums is None else sums + part
+        for m, n in enumerate(group):
+            which, place = targets[n]
+            for q in range(2):
+                total = sums[m * size : (m + 1) * size, q * width : (q + 1) * width]
+                if not got:
+                    outs[which][place, q] = total.astype(outs[which].dtype)
+                start = 0
+                for ref in got:
+                    count = ref.shape[2]
+                    added = total[start : start + count] + ref[n, q].astype(jnp.float32)
+                    outs[which][place, q, pl.ds(start, count)] = added.astype(outs[which].dtype)
+                    start += count
 
 
 def finish_kernel(pieces, momenta, rows, scale, place_ref, *refs):
@@ -217,19 +227,21 @@
 
 
 def order(last):
-    steps = [("left", (1, 0)), ("left", (1, 1)), ("xy", 0), ("pass", 1), ("left_z", 1), ("z", 0)]
-    steps += [("left", (0, 0)), ("left", (0, 1)), ("pass", 2), ("left_z", 0)]
+    steps = [("left", (1, 0)), ("left", (1, 1)), ("xy", 0), ("halo", 0), ("pass", 1), ("left_z", 1), ("z", 0)]
+    steps += [("left", (0, 0)), ("wait", 0), ("pass", 2), ("left", (0, 1)), ("left_z", 0)]
+    if last > 1:
+        steps.append(("away", 1))
     for n in range(max(last, 1)):
-        if n + 1 < last:
-            steps.append(("away", n + 1))
-        elif n + 1 == last:
-            steps += [("direct", 1), ("direct", 0)]
+        if n + 1 == last:
+            steps.append(("direct", last))
+        if n + 2 < last:
+            steps.append(("away", n + 2))
         steps.append(("home", n))
+        if n + 3 <= last:
+            steps.append(("pass", n + 3))
         if n > 0:
             steps.append(("finish", n - 1))
-        if n + 1 < last:
-            steps += [("pass", n + 3)] if n + 3 <= last else []
-    return steps + [("finish", n) for n in range(max(last - 1, 0), last + 1)]
+    return steps + [("finish", last)] + ([("finish", last - 1)] if last else [])
 
 
 def on_device(vectors, links, dirs, moms):
@@ -263,26 +275,21 @@
     flat = after(vectors.reshape(count, span), other_links, below, two_below)
     other = lax.ppermute(flat, "gz", across)
 
-    edge_shape = jax.ShapeDtypeStruct((chips * rows, 6 * PLANE), jnp.bfloat16)
-    same, cross = pl.pallas_call(
+    edge = pl.pallas_call(
         functools.partial(edge_kernel, sites),
         grid_spec=pltpu.PrefetchScalarGridSpec(
             num_scalar_prefetch=1,
             grid=(chips,),
-            in_specs=[
-                pl.BlockSpec((rows, span), lambda n, place: (n * CORES + place[1], 0)),
-                pl.BlockSpec((rows, span), lambda n, place: (n * CORES + 1 - place[1], 0)),
-            ],
-            out_specs=[pl.BlockSpec((rows, 6 * PLANE), lambda n, place: (n, 0))] * 2,
+            in_specs=[pl.BlockSpec((count // chips, span), lambda n, place: (n, 0))],
+            out_specs=pl.BlockSpec((count // chips, 6 * PLANE), lambda n, place: (n, 0)),
         ),
-        out_shape=[edge_shape] * 2,
+        out_shape=jax.ShapeDtypeStruct((count, 6 * PLANE), jnp.bfloat16),
         compiler_params=params,
         cost_estimate=cost(1e9),
         name="edges",
-    )(place, flat, flat)
+    )(place, flat)
     step = lambda i: (i - CORES if i % CORES == 0 else i + CORES) % slabs
-    first = lax.ppermute(same, "gz", [(i, step(i)) for i in range(slabs)])
-    second = lax.ppermute(cross, "gz", [(i, step(i) ^ 1) for i in range(slabs)])
+    halo = {0: lax.ppermute(edge, "gz", [(i, step(i)) for i in range(slabs)])}
 
     phase_rows = 2 * 3 * 2 * momenta
     phases = pl.pallas_call(
@@ -301,8 +308,7 @@
 
     def left_specs(odd):
         mine = lambda n, place: ((place[0] ^ (2 * n + odd)) * CORES + place[1], 0)
-        halo = lambda n, place: (place[0] ^ (2 * n + odd), 0)
-        return pl.BlockSpec((rows, span), mine), pl.BlockSpec((rows, 6 * PLANE), halo)
+        return pl.BlockSpec((rows, span), mine), pl.BlockSpec((rows, 6 * PLANE), mine)
 
     def left_xy(odd, which, vecs, table, place):
         return pl.pallas_call(
@@ -316,7 +322,7 @@
             ),
             out_shape=left_shape,
             compiler_params=params,
-            cost_estimate=cost(4e9 if odd == 0 else 1e9),
+            cost_estimate=cost(4e9 if odd == 0 else 0.5e9),
             name="left_xy",
         )(place, vecs, table, phases)
 
@@ -338,43 +344,45 @@
             compiler_params=params,
             cost_estimate=cost(5e9),
             name="left_z",
-        )(place, flat, other, first, second, tables, other_tables, phases, *sides)
-
-    def product(sides, mine, theirs, targets, kinds, first_row=0, size=left_rows, received=()):
+        )(place, flat, other, halo[0], halo[1], tables, other_tables, phases, *sides)
+
+    def product(sides, mine, theirs, targets, kinds, first_row=0, size=left_rows, received=(), work=7e9):
         width = sum(piece.shape[0] for piece in mine)
         kept = pl.BlockSpec(memory_space=pl.ANY)
         in_vmem = pl.BlockSpec(memory_space=pltpu.VMEM)
         chunks = [sum(which == n for which, _ in targets) for n in range(len(kinds))]
+        pairs = len(sides) // 2
         return pl.pallas_call(
-            functools.partial(product_kernel, sites, half, first_row, size, len(mine), len(received), targets),
-            in_specs=[kept] * (2 * len(mine) + 2) + [in_vmem] * len(received),
+            functools.partial(product_kernel, sites, half, first_row, size, len(mine), pairs, len(received), targets),
+            in_specs=[kept] * (2 * len(mine) + len(sides)) + [in_vmem] * len(received),
             out_specs=[in_vmem] * len(kinds),
             out_shape=[jax.ShapeDtypeStruct((n, 2, size, width), kind) for n, kind in zip(chunks, kinds)],
             scratch_shapes=[
                 pltpu.VMEM((2 * width, 2 * span), jnp.bfloat16),
-                pltpu.VMEM((half * size, 2 * span), jnp.bfloat16),
+                pltpu.VMEM((pairs * half * size, 2 * span), jnp.bfloat16),
                 pltpu.SemaphoreType.DMA((2, len(mine))),
-                pltpu.SemaphoreType.DMA((2, half)),
+                pltpu.SemaphoreType.DMA((2, pairs * half)),
             ],
             compiler_params=params,
-            cost_estimate=cost(7e9 * size / left_rows),
+            cost_estimate=cost(work),
             name="product",
         )(*mine, *theirs, *sides, *received)
 
-    def product_away(sides, right, *rows):
-        (away,) = product(sides, *right, [(0, n) for n in range(half)], [jnp.bfloat16], *rows)
+    def product_away(sides, right, first_row, size, work):
+        (away,) = product(sides, *right, [(0, n) for n in range(half)], [jnp.bfloat16], first_row, size, work=work)
         return away, to_chip(away, 1)
 
-    def product_home(sides, right, received):
+    def product_home(sides, right, received, work):
         if half == 1:
-            return product(sides, *right, [(0, 0)], [jnp.float32], received=received)
+            return product(sides, *right, [(0, 0)], [jnp.float32], received=received, work=work)
         targets = [(n % 2, n // 2) for n in range(half)]
-        return product(sides, *right, targets, [jnp.float32, jnp.bfloat16], received=received)
-
-    def product_direct(sides, right, odd):
-        kinds = [jnp.float32 if n == 0 and not odd else jnp.bfloat16 for n in range(half)]
-        outs = product(sides, *right, [(n, 0) for n in range(half)], kinds)
-        return outs, [out if 2 * n + odd == 0 else to_chip(out, 2 * n + odd) for n, out in enumerate(outs)]
+        return product(sides, *right, targets, [jnp.float32, jnp.bfloat16], received=received, work=work)
+
+    def product_direct(odd, even, right):
+        kinds = [jnp.bfloat16] * half + [jnp.float32] + [jnp.bfloat16] * (half - 1)
+        outs = product([*odd, *even], *right, [(n, 0) for n in range(chips)], kinds, work=1e9)
+        far = [2 * n + 1 for n in range(half)] + [2 * n for n in range(half)]
+        return outs[half], [out if s == 0 else to_chip(out, s) for s, out in zip(far, outs)]
 
     scale = 1.0 / math.sqrt(3.0 * sites * slabs)
     spots = 2 * (dirs % 3) + dirs // 3
@@ -400,7 +408,7 @@
             out_shape=out_shape,
             input_output_aliases=aliases,
             compiler_params=params,
-            cost_estimate=cost(3e9),
+            cost_estimate=cost(0.1e9),
             name="finish",
         )(at, *operands)
 
@@ -484,27 +492,29 @@
             done = sides[n][0]
         elif step == "pass":
             pass_on(n, done)
+        elif step == "halo":
+            halo[1] = lax.ppermute(after(halo[0], done), "gz", across)
+        elif step == "wait":
+            done = after(done, received[n][0])
         elif step == "finish":
             result = done = finish([after(sums[n][0], done)] + sums[n][1:], own_columns(n), result)
         else:
             even = [after(sides[0][0], done), sides[0][1]]
             odd = [after(sides[1][0], done), sides[1][1]]
             if step == "xy":
-                done, arrived = product_away(odd, right[n], 0, flat_rows)
+                done, arrived = product_away(odd, right[n], 0, flat_rows, 1e9)
                 received[n].append(arrived)
             elif step == "z":
-                done, arrived = product_away(odd, right[n], flat_rows, left_rows - flat_rows)
+                done, arrived = product_away(odd, right[n], flat_rows, left_rows - flat_rows, 2.5e9)
                 received[n].append(arrived)
             elif step == "away":
-                done, arrived = product_away(odd, right[n], 0, left_rows)
+                done, arrived = product_away(odd, right[n], 0, left_rows, 5e9)
                 received[n] = [arrived]
             elif step == "home":
-                outs = product_home(even, right[n], received[n])
+                outs = product_home(even, right[n], received[n], 2e9 if n == 0 else 10e9)
                 sums[n], done = reduce_more(*outs), outs[0]
             elif step == "direct":
-                outs, pieces = product_direct(odd if n else even, right[last], n)
-                sums[last] = pieces + sums.get(last, []) if n == 0 else sums.get(last, []) + pieces
-                done = outs[0]
+                done, sums[n] = product_direct(odd, even, right[n])
 
     for step, n in order(last):
         run(step, n)

time: 202 us -> 202 us (level)
  the two profiles are of different devices: /device:TPU:17 before, /device:TPU:0 now
where the time goes in v1:
time: 202 us; the launch traced here: 199 us
  Pallas kernels  106 us (52%)
  waiting for transfers between devices  55 us (27%)
  starting transfers between devices  28.1 us (14%)
  local copies, waits for them, and re-layouts  9.15 us (5%)
    pallas_call x8, Pallas kernels, product(): pl.pallas_call(functools.partial(product_kernel, sites, half, first_row,...  71 us
    ppermute x10, waiting for transfers between devices, to_chip(): lax.ppermute(array, 'gz', [(i, i ^ CORES * bit) for i in range(slabs)])  46.6 us
    pallas_call x4, Pallas kernels, left_xy(): pl.pallas_call(functools.partial(left_xy_kernel, momenta, rows, sites, wh...  18.8 us
    ppermute x10, starting transfers between devices, to_chip(): lax.ppermute(array, 'gz', [(i, i ^ CORES * bit) for i in range(slabs)])  14.2 us
    ppermute x5, waiting for transfers between devices, from_group(): return lax.ppermute(array, 'vec', [(i, i ^ turn) for i in range(groups)])  8.35 us
    pallas_call x2, Pallas kernels, left_z(): pl.pallas_call(functools.partial(left_z_kernel, momenta, rows, sites), gr...  7.49 us
    pallas_call x4, Pallas kernels, finish(): pl.pallas_call(functools.partial(finish_kernel, len(pieces), momenta, row...  6.68 us
    ppermute x5, starting transfers between devices, from_group(): return lax.ppermute(array, 'vec', [(i, i ^ turn) for i in range(groups)])  6.65 us
  transfers between devices with their start and end apart: 24, of which 7 were waited for; matrix products, arithmetic and copies ran while one was open for 2% of the time, Pallas kernels for 52%

profile of v1, /device:TPU:0, one launch (start us, length us, event | category | flops | bytes accessed | tf_op | source)
XLA Modules:
  0.0 198.7 jit_solution(17489139677049146282)
XLA Ops:
  0.0 1.0 reshape.7
  1.0 0.5 collective-permute-start.1
  1.5 2.6 %collective-permute-start.2 = (f32[18,256]{1,0:T(8,128)S(1)}, f32[18,256]{1,0:T(8,128)S(1)}, u32[]{:S(2)}, u32[]{:S(2)}) collective-permute-start(f32[18,256]{1,0:T(8,128)S(1)} %get-tuple-element.92), channel_id=1, source_target_pairs={{0,2},{1,3},{2,4},{3,5},{4,6},{5,7},{6,0},{7,1},{8,10},{9,11},{10,... | collective-permute-start | bytes 55304 | tf_op jit(solution)/shard_map/ppermute | solution.py:266
  4.1 1.3 collective-permute-start
  5.5 0.1 pad_add_fusion.1.place_ref
  5.6 0.7 copy-done.9
  6.2 0.9 phases.1.phase_ref
  7.2 4.0 %reshape.6.vec_ref.refs_0_.own_ref = bf16[256,3072]{1,0:T(8,128)(2,1)S(1)} reshape(bf16[256,3,2,512]{3,2,1,0:T(2,128)(2,1)} %param.4) | data formatting | bytes 3145728 | tf_op jit(solution)/shard_map/reshape | solution.py:275
  11.2 0.0 collective-permute-done.1
  11.2 0.0 collective-permute-done.2
  11.2 0.1 collective-permute-start.4
  11.3 0.7 edges.1
  12.0 2.3 %collective-permute-start.7 = (bf16[256,1536]{1,0:T(8,128)(2,1)S(1)}, bf16[256,1536]{1,0:T(8,128)(2,1)S(1)}, u32[]{:S(2)}, u32[]{:S(2)}) collective-permute-start(bf16[256,1536]{1,0:T(8,128)(2,1)S(1)} %edges.1), channel_id=1, source_target_pairs={{0,6},{1,3},{2,0},{3,5},{4,2},{5,7},{6,4},{7,1},{8,14},{9,11},{10,... | collective-permute-start | bytes 2359304 | tf_op jit(solution)/shard_map/ppermute | solution.py:292
  14.3 0.1 fusion.2
  14.5 1.6 collective-permute-start.5
  16.0 1.5 collective-permute-start.3
  17.5 4.8 %left_xy.4.refs_2_.refs_0_ = bf16[2,384,3072]{2,1,0:T(8,128)(2,1)} custom-call(s32[2]{0:T(128)S(1)} %pad_add_fusion.1.place_ref, bf16[256,3072]{1,0:T(8,128)(2,1)S(1)} %reshape.6.vec_ref.refs_0_.own_ref, f32[4,18,512]{2,1,0:T(8,128)S(1)} %pad_maximum_fusion.link_ref, f32[2,24,512]{2,1,0:T(8,128)S(1)} %phases.1.phase_ref), custom_call_target="tpu_custom_call" | custom-call | flops 500000000 | bytes 1024 | tf_op jit(solution)/shard_map/left_xy/pallas_call | solution.py:314
  22.4 4.5 %left_xy.5.refs_3_.refs_1_ = bf16[2,384,3072]{2,1,0:T(8,128)(2,1)} custom-call(s32[2]{0:T(128)S(1)} %pad_add_fusion.1.place_ref, bf16[256,3072]{1,0:T(8,128)(2,1)S(1)} %collective-permute-done.4.vec_ref.refs_1_.other_ref, f32[4,18,512]{2,1,0:T(8,128)S(1)} %pad_maximum_fusion.1.link_ref.other_link_ref, f32[2,24,512]{2,1,0:T(8,128)S(1)} %phases.1.phase_ref), custom_call_target="tpu_custom_call" | custom-call | flops 500000000 | bytes 1024 | tf_op jit(solution)/shard_map/left_xy/pallas_call | solution.py:314
  27.0 6.2 %product.8 = bf16[2,2,256,256]{3,2,1,0:T(8,128)(2,1)S(1)} custom-call(bf16[256,3072]{1,0:T(8,128)(2,1)S(1)} %reshape.6.vec_ref.refs_0_.own_ref, bf16[256,3072]{1,0:T(8,128)(2,1)S(1)} %collective-permute-done.4.vec_ref.refs_1_.other_ref, bf16[2,384,3072]{2,1,0:T(8,128)(2,1)} %left_xy.4.refs_2_.refs_0_, bf16[2,384,3072]{2,1,0:T(8,128)(2,1)} %left_xy.5.refs_3_.refs_1_), custom_call_target="tpu_custom_call" | custom-call | flops 1000000000 | bytes 1024 | tf_op jit(solution)/shard_map/product/pallas_call | solution.py:355
  33.1 0.4 collective-permute-start.8
  33.5 0.3 collective-permute-start.9
  33.8 0.9 collective-permute-done.3
  34.7 0.1 constant_dynamic-update-slice_fusion.1
  34.8 0.1 constant_dynamic-update-slice_fusion.refs_0_
  34.9 0.0 copy-start.4
  34.9 0.6 collective-permute-start.10
  35.5 1.5 collective-permute-start.6
  37.0 3.7 %left_z.2 = (bf16[2,384,3072]{2,1,0:T(8,128)(2,1)}, bf16[2,384,3072]{2,1,0:T(8,128)(2,1)}) custom-call(s32[2]{0:T(128)S(1)} %pad_add_fusion.1.place_ref, bf16[256,3072]{1,0:T(8,128)(2,1)S(1)} %reshape.6.vec_ref.refs_0_.own_ref, bf16[256,3072]{1,0:T(8,128)(2,1)S(1)} %collective-permute-done.4.vec_ref.refs_1_.other_ref, ...), custom_call_target="tpu_custom_call", output_to_operand_aliasing={{0}: (8, {}), {1}: (9, {})} | custom-call | flops 5000000000 | bytes 1024 | tf_op jit(solution)/shard_map/left_z/pallas_call | solution.py:332
  40.7 3.9 %product.9 = bf16[2,2,128,256]{3,2,1,0:T(8,128)(2,1)S(1)} custom-call(bf16[256,3072]{1,0:T(8,128)(2,1)S(1)} %reshape.6.vec_ref.refs_0_.own_ref, bf16[256,3072]{1,0:T(8,128)(2,1)S(1)} %collective-permute-done.4.vec_ref.refs_1_.other_ref, bf16[2,384,3072]{2,1,0:T(8,128)(2,1)} %get-tuple-element.76.refs_2_, bf16[2,384,3072]{2,1,0:T(8,128)(2,1)} %get-tuple-element.58.refs_3_), custom_call_target="tpu_custom_call" | custom-call | flops 2500000000 | bytes 1024 | tf_op jit(solution)/shard_map/product/pallas_call | solution.py:355
  44.6 5.0 %left_xy.6.refs_0_ = bf16[2,384,3072]{2,1,0:T(8,128)(2,1)} custom-call(s32[2]{0:T(128)S(1)} %pad_add_fusion.1.place_ref, bf16[256,3072]{1,0:T(8,128)(2,1)S(1)} %reshape.6.vec_ref.refs_0_.own_ref, f32[4,18,512]{2,1,0:T(8,128)S(1)} %pad_maximum_fusion.link_ref, f32[2,24,512]{2,1,0:T(8,128)S(1)} %phases.1.phase_ref), custom_call_target="tpu_custom_call" | custom-call | flops 4000000000 | bytes 1024 | tf_op jit(solution)/shard_map/left_xy/pallas_call | solution.py:314
  49.6 5.3 %collective-permute-done.6 = bf16[128,3072]{1,0:T(8,128)(2,1)S(1)} collective-permute-done((bf16[128,3072]{1,0:T(8,128)(2,1)S(1)}, bf16[128,3072]{1,0:T(8,128)(2,1)S(1)}, u32[]{:S(2)}, u32[]{:S(2)}) %collective-permute-start.6) | collective-permute-done | bytes 786464 | tf_op jit(solution)/shard_map/ppermute | solution.py:419
  54.9 0.1 constant_dynamic-update-slice_fusion.3
  55.0 0.1 constant_dynamic-update-slice_fusion.2.refs_0_
  55.0 0.1 collective-permute-start.11
  55.1 1.3 collective-permute-start.14
  56.4 4.5 %left_xy.7.refs_1_ = bf16[2,384,3072]{2,1,0:T(8,128)(2,1)} custom-call(s32[2]{0:T(128)S(1)} %pad_add_fusion.1.place_ref, bf16[256,3072]{1,0:T(8,128)(2,1)S(1)} %collective-permute-done.4.vec_ref.refs_1_.other_ref, f32[4,18,512]{2,1,0:T(8,128)S(1)} %pad_maximum_fusion.1.link_ref.other_link_ref, f32[2,24,512]{2,1,0:T(8,128)S(1)} %phases.1.phase_ref), custom_call_target="tpu_custom_call" | custom-call | flops 4000000000 | bytes 1024 | tf_op jit(solution)/shard_map/left_xy/pallas_call | solution.py:314
  60.9 1.4 collective-permute-start.12
  62.4 3.8 %left_z.3 = (bf16[2,384,3072]{2,1,0:T(8,128)(2,1)}, bf16[2,384,3072]{2,1,0:T(8,128)(2,1)}) custom-call(s32[2]{0:T(128)S(1)} %pad_add_fusion.1.place_ref, bf16[256,3072]{1,0:T(8,128)(2,1)S(1)} %reshape.6.vec_ref.refs_0_.own_ref, bf16[256,3072]{1,0:T(8,128)(2,1)S(1)} %collective-permute-done.4.vec_ref.refs_1_.other_ref, ...), custom_call_target="tpu_custom_call", output_to_operand_aliasing={{0}: (8, {}), {1}: (9, {})} | custom-call | flops 5000000000 | bytes 1024 | tf_op jit(solution)/shard_map/left_z/pallas_call | solution.py:332
  66.1 10.4 %product.10 = bf16[2,2,384,256]{3,2,1,0:T(8,128)(2,1)} custom-call(bf16[256,3072]{1,0:T(8,128)(2,1)S(1)} %constant_dynamic-update-slice_fusion.refs_0_, bf16[256,3072]{1,0:T(8,128)(2,1)} %collective-permute-done.13.refs_1_, bf16[2,384,3072]{2,1,0:T(8,128)(2,1)} %get-tuple-element.76.refs_2_, bf16[2,384,3072]{2,1,0:T(8,128)(2,1)} %get-tuple-element.58.refs_3_), custom_call_target="tpu_custom_call" | custom-call | flops 5000000000 | bytes 1024 | tf_op jit(solution)/shard_map/product/pallas_call | solution.py:355
  76.5 0.9 collective-permute-start.16
  77.4 8.7 %product.11 = bf16[2,2,384,256]{3,2,1,0:T(8,128)(2,1)S(1)} custom-call(bf16[256,3072]{1,0:T(8,128)(2,1)S(1)} %constant_dynamic-update-slice_fusion.2.refs_0_, bf16[256,3072]{1,0:T(8,128)(2,1)S(1)} %collective-permute-done.11.refs_1_, bf16[2,384,3072]{2,1,0:T(8,128)(2,1)} %get-tuple-element.76.refs_2_, bf16[2,384,3072]{2,1,0:T(8,128)(2,1)} %get-tuple-element.58.refs_3_), custom_call_target="tpu_custom_call" | custom-call | flops 5000000000 | bytes 1024 | tf_op jit(solution)/shard_map/product/pallas_call | solution.py:355
  86.1 0.9 copy-done.8
  87.0 8.3 %product.12 = (f32[1,2,384,256]{3,2,1,0:T(8,128)S(1)}, bf16[1,2,384,256]{3,2,1,0:T(8,128)(2,1)S(1)}) custom-call(bf16[256,3072]{1,0:T(8,128)(2,1)S(1)} %reshape.6.vec_ref.refs_0_.own_ref, bf16[256,3072]{1,0:T(8,128)(2,1)S(1)} %collective-permute-done.4.vec_ref.refs_1_.other_ref, bf16[2,384,3072]{2,1,0:T(8,128)(2,1)} %get-tuple-element.79.refs_2_.refs_4_, ...), custom_call_target="tpu_custom_call" | custom-call | flops 2000000000 | bytes 1024 | tf_op jit(solution)/shard_map/product/pallas_call | solution.py:355
  95.3 0.9 copy-done
  96.2 2.1 %collective-permute-done.12.refs_0_ = bf16[256,3072]{1,0:T(8,128)(2,1)S(1)} collective-permute-done((bf16[256,3072]{1,0:T(8,128)(2,1)S(1)}, bf16[256,3072]{1,0:T(8,128)(2,1)S(1)}, u32[]{:S(2)}, u32[]{:S(2)}) %collective-permute-start.12) | collective-permute-done | bytes 1572896 | tf_op jit(solution)/shard_map/ppermute | solution.py:419
  98.3 0.1 pad_add_fusion.4
  98.4 0.8 collective-permute-start.18
  99.2 2.2 %collective-permute-start.17 = (bf16[1,2,384,256]{3,2,1,0:T(8,128)(2,1)S(1)}, bf16[1,2,384,256]{3,2,1,0:T(8,128)(2,1)S(1)}, u32[]{:S(2)}, u32[]{:S(2)}) collective-permute-start(bf16[1,2,384,256]{3,2,1,0:T(8,128)(2,1)S(1)} %get-tuple-element.75), channel_id=1, source_target_pairs={{0,4},{1,5},{2,6},{3,7},{4,0},{5,1},{6,2},{7,3},{8,12},{9,13},{10,... | collective-permute-start | bytes 1179656 | tf_op jit(solution)/shard_map/ppermute | solution.py:416
  101.4 1.4 copy-done.5
  102.8 10.8 %product.13 = (f32[1,2,384,256]{3,2,1,0:T(8,128)S(1)}, bf16[1,2,384,256]{3,2,1,0:T(8,128)(2,1)S(1)}) custom-call(bf16[256,3072]{1,0:T(8,128)(2,1)S(1)} %copy-done.5, bf16[256,3072]{1,0:T(8,128)(2,1)} %collective-permute-done.13.refs_1_, bf16[2,384,3072]{2,1,0:T(8,128)(2,1)} %get-tuple-element.79.refs_2_.refs_4_, ...), custom_call_target="tpu_custom_call" | custom-call | flops 10000000000 | bytes 1024 | tf_op jit(solution)/shard_map/product/pallas_call | solution.py:355
  113.6 0.8 collective-permute-start.20
  114.4 11.3 %collective-permute-done.17.refs_1_ = bf16[1,2,384,256]{3,2,1,0:T(8,128)(2,1)S(1)} collective-permute-done((bf16[1,2,384,256]{3,2,1,0:T(8,128)(2,1)S(1)}, bf16[1,2,384,256]{3,2,1,0:T(8,128)(2,1)S(1)}, u32[]{:S(2)}, u32[]{:S(2)}) %collective-permute-start.17) | collective-permute-done | bytes 393248 | tf_op jit(solution)/shard_map/ppermute | solution.py:416
  125.7 1.6 finish.4.refs_2_
  127.4 14.5 %product.14 = (bf16[1,2,384,256]{3,2,1,0:T(8,128)(2,1)S(1)}, bf16[1,2,384,256]{3,2,1,0:T(8,128)(2,1)S(1)}, f32[1,2,384,256]{3,2,1,0:T(8,128)S(1)}, bf16[1,2,384,256]{3,2,1,0:T(8,128)(2,1)S(1)}) custom-call(bf16[256,3072]{1,0:T(8,128)(2,1)S(1)} %collective-permute-done.12.refs_0_, bf16[256,3072]{1,0:T(8,128)(2,1)S(1)} %collective-permute-done.15.refs_1_, ...), custom_call_target="tpu_custom_call" | custom-call | flops 1000000000 | bytes 1024 | tf_op jit(solution)/shard_map/product/pallas_call | solution.py:355
  141.9 3.0 %collective-permute-start.19 = (bf16[1,2,384,256]{3,2,1,0:T(8,128)(2,1)S(1)}, bf16[1,2,384,256]{3,2,1,0:T(8,128)(2,1)S(1)}, u32[]{:S(2)}, u32[]{:S(2)}) collective-permute-start(bf16[1,2,384,256]{3,2,1,0:T(8,128)(2,1)S(1)} %get-tuple-element.81), channel_id=1, source_target_pairs={{0,2},{1,3},{2,0},{3,1},{4,6},{5,7},{6,4},{7,5},{8,10},{9,11},{10,... | collective-permute-start | bytes 1179656 | tf_op jit(solution)/shard_map/ppermute | solution.py:416
  144.9 1.9 collective-permute-start.21
  146.8 8.3 %product.15 = (f32[1,2,384,256]{3,2,1,0:T(8,128)S(1)}, bf16[1,2,384,256]{3,2,1,0:T(8,128)(2,1)S(1)}) custom-call(bf16[256,3072]{1,0:T(8,128)(2,1)S(1)} %copy-done.3, bf16[256,3072]{1,0:T(8,128)(2,1)S(1)} %copy-done.7, bf16[2,384,3072]{2,1,0:T(8,128)(2,1)} %get-tuple-element.79.refs_2_.refs_4_, bf16[2,384,3072]{2,1,0:T(8,128)(2,1)} %get-tuple-element.69.refs_3_.refs_5_, ...), custom_call_target="tpu_custom_call" | custom-call | flops 10000000000 | bytes 1024 | tf_op jit(solution)/shard_map/product/pallas_call | solution.py:355
  155.2 3.0 %collective-permute-start.23 = (bf16[1,2,384,256]{3,2,1,0:T(8,128)(2,1)S(1)}, bf16[1,2,384,256]{3,2,1,0:T(8,128)(2,1)S(1)}, u32[]{:S(2)}, u32[]{:S(2)}) collective-permute-start(bf16[1,2,384,256]{3,2,1,0:T(8,128)(2,1)S(1)} %get-tuple-element.88), channel_id=1, source_target_pairs={{0,4},{1,5},{2,6},{3,7},{4,0},{5,1},{6,2},{7,3},{8,12},{9,13},{10,... | collective-permute-start | bytes 1179656 | tf_op jit(solution)/shard_map/ppermute | solution.py:416
  158.1 1.6 finish.5.refs_4_
  159.8 5.6 %collective-permute-done.21.refs_1_ = bf16[1,2,384,256]{3,2,1,0:T(8,128)(2,1)S(1)} collective-permute-done((bf16[1,2,384,256]{3,2,1,0:T(8,128)(2,1)S(1)}, bf16[1,2,384,256]{3,2,1,0:T(8,128)(2,1)S(1)}, u32[]{:S(2)}, u32[]{:S(2)}) %collective-permute-start.21) | collective-permute-done | bytes 393248 | tf_op jit(solution)/shard_map/ppermute | solution.py:416
  165.4 24.8 %collective-permute-done.22.refs_3_ = bf16[1,2,384,256]{3,2,1,0:T(8,128)(2,1)S(1)} collective-permute-done((bf16[1,2,384,256]{3,2,1,0:T(8,128)(2,1)S(1)}, bf16[1,2,384,256]{3,2,1,0:T(8,128)(2,1)S(1)}, u32[]{:S(2)}, u32[]{:S(2)}) %collective-permute-start.22) | collective-permute-done | bytes 393248 | tf_op jit(solution)/shard_map/ppermute | solution.py:416
  190.2 1.8 finish.6.refs_2_
  192.0 4.9 %collective-permute-done.23.refs_1_ = bf16[1,2,384,256]{3,2,1,0:T(8,128)(2,1)S(1)} collective-permute-done((bf16[1,2,384,256]{3,2,1,0:T(8,128)(2,1)S(1)}, bf16[1,2,384,256]{3,2,1,0:T(8,128)(2,1)S(1)}, u32[]{:S(2)}, u32[]{:S(2)}) %collective-permute-start.23) | collective-permute-done | bytes 393248 | tf_op jit(solution)/shard_map/ppermute | solution.py:416
  196.8 1.6 finish.7
  (43 shorter events, 0.2 us)
Async XLA Ops:
  1.0 10.2 %collective-permute-start.1 = (f32[18,256]{1,0:T(8,128)S(1)}, f32[18,256]{1,0:T(8,128)S(1)}, u32[]{:S(2)}, u32[]{:S(2)}) collective-permute-start(f32[18,256]{1,0:T(8,128)S(1)} %get-tuple-element.92), channel_id=1, source_target_pairs={{0,1},{1,2},{2,3},{3,4},{4,5},{5,6},{6,7},{7,0},{8,9},{9,10},{10,1... | collective-permute-start | bytes 55304 | tf_op jit(solution)/shard_map/ppermute | solution.py:265
  1.5 9.7 %collective-permute-start.2 = (f32[18,256]{1,0:T(8,128)S(1)}, f32[18,256]{1,0:T(8,128)S(1)}, u32[]{:S(2)}, u32[]{:S(2)}) collective-permute-start(f32[18,256]{1,0:T(8,128)S(1)} %get-tuple-element.92), channel_id=1, source_target_pairs={{0,2},{1,3},{2,4},{3,5},{4,6},{5,7},{6,0},{7,1},{8,10},{9,11},{10,... | collective-permute-start | bytes 55304 | tf_op jit(solution)/shard_map/ppermute | solution.py:266
  4.1 7.1 %collective-permute-start = (f32[3,18,512]{2,1,0:T(8,128)S(1)}, f32[3,18,512]{2,1,0:T(8,128)S(1)}, u32[]{:S(2)}, u32[]{:S(2)}) collective-permute-start(f32[3,18,512]{2,1,0:T(8,128)S(1)} %reshape.7), channel_id=1, source_target_pairs={{0,1},{1,0},{2,3},{3,2},{4,5},{5,4},{6,7},{7,6},{8,9},{9,8},{10,11... | collective-permute-start | bytes 331784 | tf_op jit(solution)/shard_map/ppermute | solution.py:264
  5.6 0.7 copy-start.9
  11.2 11.2 %collective-permute-start.4 = (bf16[256,3072]{1,0:T(8,128)(2,1)S(1)}, bf16[256,3072]{1,0:T(8,128)(2,1)S(1)}, u32[]{:S(2)}, u32[]{:S(2)}) collective-permute-start(bf16[256,3072]{1,0:T(8,128)(2,1)S(1)} %reshape.6.vec_ref.refs_0_.own_ref), channel_id=1, source_target_pairs={{0,1},{1,0},{2,3},{3,2},{4,5},{5,4},{6,7},{7,6},{8,9},{9,8},{10,11... | collective-permute-start | bytes 4718600 | tf_op jit(solution)/shard_map/ppermute | solution.py:276
  12.0 21.1 %collective-permute-start.7 = (bf16[256,1536]{1,0:T(8,128)(2,1)S(1)}, bf16[256,1536]{1,0:T(8,128)(2,1)S(1)}, u32[]{:S(2)}, u32[]{:S(2)}) collective-permute-start(bf16[256,1536]{1,0:T(8,128)(2,1)S(1)} %edges.1), channel_id=1, source_target_pairs={{0,6},{1,3},{2,0},{3,5},{4,2},{5,7},{6,4},{7,1},{8,14},{9,11},{10,... | collective-permute-start | bytes 2359304 | tf_op jit(solution)/shard_map/ppermute | solution.py:292
  14.5 19.3 %collective-permute-start.5 = (bf16[128,3072]{1,0:T(8,128)(2,1)S(1)}, bf16[128,3072]{1,0:T(8,128)(2,1)S(1)}, u32[]{:S(2)}, u32[]{:S(2)}) collective-permute-start(bf16[128,3072]{1,0:T(8,128)(2,1)S(1)} %get-tuple-element.89), channel_id=1, source_target_pairs={{0,16},{8,24},{16,0},{24,8},{1,17},{9,25},{17,1},{25,9},{2,18},{10... | collective-permute-start | bytes 2359304 | tf_op jit(solution)/shard_map/ppermute | solution.py:419
  16.0 18.7 %collective-permute-start.3 = (bf16[128,3072]{1,0:T(8,128)(2,1)S(1)}, bf16[128,3072]{1,0:T(8,128)(2,1)S(1)}, u32[]{:S(2)}, u32[]{:S(2)}) collective-permute-start(bf16[128,3072]{1,0:T(8,128)(2,1)S(1)} %get-tuple-element.89), channel_id=1, source_target_pairs={{0,8},{8,0},{16,24},{24,16},{1,9},{9,1},{17,25},{25,17},{2,10},{10... | collective-permute-start | bytes 2359304 | tf_op jit(solution)/shard_map/ppermute | solution.py:419
  33.1 3.9 %collective-permute-start.8 = (bf16[256,1536]{1,0:T(8,128)(2,1)S(1)}, bf16[256,1536]{1,0:T(8,128)(2,1)S(1)}, u32[]{:S(2)}, u32[]{:S(2)}) collective-permute-start(bf16[256,1536]{1,0:T(8,128)(2,1)S(1)} %collective-permute-done.7.first_ref), channel_id=1, source_target_pairs={{0,1},{1,0},{2,3},{3,2},{4,5},{5,4},{6,7},{7,6},{8,9},{9,8},{10,11... | collective-permute-start | bytes 2359304 | tf_op jit(solution)/shard_map/ppermute | solution.py:496
  33.5 16.1 %collective-permute-start.9 = (bf16[2,2,256,256]{3,2,1,0:T(8,128)(2,1)S(1)}, bf16[2,2,256,256]{3,2,1,0:T(8,128)(2,1)S(1)}, u32[]{:S(2)}, u32[]{:S(2)}) collective-permute-start(bf16[2,2,256,256]{3,2,1,0:T(8,128)(2,1)S(1)} %product.8), channel_id=1, source_target_pairs={{0,2},{1,3},{2,0},{3,1},{4,6},{5,7},{6,4},{7,5},{8,10},{9,11},{10,... | collective-permute-start | bytes 1572872 | tf_op jit(solution)/shard_map/ppermute | solution.py:416
  34.9 31.3 %copy-start.4 = (bf16[256,3072]{1,0:T(8,128)(2,1)}, bf16[256,3072]{1,0:T(8,128)(2,1)S(1)}, u32[]{:S(2)}) copy-start(bf16[256,3072]{1,0:T(8,128)(2,1)S(1)} %constant_dynamic-update-slice_fusion.refs_0_) | copy-start | bytes 4718596
  34.9 20.1 %collective-permute-start.10 = (bf16[128,3072]{1,0:T(8,128)(2,1)S(1)}, bf16[128,3072]{1,0:T(8,128)(2,1)S(1)}, u32[]{:S(2)}, u32[]{:S(2)}) collective-permute-start(bf16[128,3072]{1,0:T(8,128)(2,1)S(1)} %get-tuple-element.53), channel_id=1, source_target_pairs={{0,16},{8,24},{16,0},{24,8},{1,17},{9,25},{17,1},{25,9},{2,18},{10... | collective-permute-start | bytes 2359304 | tf_op jit(solution)/shard_map/ppermute | solution.py:419
  35.5 19.4 %collective-permute-start.6 = (bf16[128,3072]{1,0:T(8,128)(2,1)S(1)}, bf16[128,3072]{1,0:T(8,128)(2,1)S(1)}, u32[]{:S(2)}, u32[]{:S(2)}) collective-permute-start(bf16[128,3072]{1,0:T(8,128)(2,1)S(1)} %get-tuple-element.53), channel_id=1, source_target_pairs={{0,8},{8,0},{16,24},{24,16},{1,9},{9,1},{17,25},{25,17},{2,10},{10... | collective-permute-start | bytes 2359304 | tf_op jit(solution)/shard_map/ppermute | solution.py:419
  37.0 29.1 %collective-permute-start.13 = (bf16[256,3072]{1,0:T(8,128)(2,1)S(1)}, bf16[256,3072]{1,0:T(8,128)(2,1)}, u32[]{:S(2)}, u32[]{:S(2)}) collective-permute-start(bf16[256,3072]{1,0:T(8,128)(2,1)S(1)} %constant_dynamic-update-slice_fusion.refs_0_), channel_id=1, source_target_pairs={{0,1},{1,0},{2,3},{3,2},{4,5},{5,4},{6,7},{7,6},{8,9},{9,8},{10,11... | collective-permute-start | bytes 4718600 | tf_op jit(solution)/shard_map/ppermute | solution.py:422
  55.0 22.4 %copy-start.2 = (bf16[256,3072]{1,0:T(8,128)(2,1)}, bf16[256,3072]{1,0:T(8,128)(2,1)S(1)}, u32[]{:S(2)}) copy-start(bf16[256,3072]{1,0:T(8,128)(2,1)S(1)} %constant_dynamic-update-slice_fusion.2.refs_0_) | copy-start | bytes 4718596
  55.0 22.4 %collective-permute-start.11 = (bf16[256,3072]{1,0:T(8,128)(2,1)S(1)}, bf16[256,3072]{1,0:T(8,128)(2,1)S(1)}, u32[]{:S(2)}, u32[]{:S(2)}) collective-permute-start(bf16[256,3072]{1,0:T(8,128)(2,1)S(1)} %constant_dynamic-update-slice_fusion.2.refs_0_), channel_id=1, source_target_pairs={{0,1},{1,0},{2,3},{3,2},{4,5},{5,4},{6,7},{7,6},{8,9},{9,8},{10,11... | collective-permute-start | bytes 4718600 | tf_op jit(solution)/shard_map/ppermute | solution.py:422
  55.1 31.9 %collective-permute-start.14 = (bf16[2,2,128,256]{3,2,1,0:T(8,128)(2,1)S(1)}, bf16[2,2,128,256]{3,2,1,0:T(8,128)(2,1)S(1)}, u32[]{:S(2)}, u32[]{:S(2)}) collective-permute-start(bf16[2,2,128,256]{3,2,1,0:T(8,128)(2,1)S(1)} %product.9), channel_id=1, source_target_pairs={{0,2},{1,3},{2,0},{3,1},{4,6},{5,7},{6,4},{7,5},{8,10},{9,11},{10,... | collective-permute-start | bytes 786440 | tf_op jit(solution)/shard_map/ppermute | solution.py:416
  60.9 37.4 %collective-permute-start.12 = (bf16[256,3072]{1,0:T(8,128)(2,1)S(1)}, bf16[256,3072]{1,0:T(8,128)(2,1)S(1)}, u32[]{:S(2)}, u32[]{:S(2)}) collective-permute-start(bf16[256,3072]{1,0:T(8,128)(2,1)S(1)} %reshape.6.vec_ref.refs_0_.own_ref), channel_id=1, source_target_pairs={{0,24},{8,16},{16,8},{24,0},{1,25},{9,17},{17,9},{25,1},{2,26},{10... | collective-permute-start | bytes 4718600 | tf_op jit(solution)/shard_map/ppermute | solution.py:419
  76.5 24.8 %collective-permute-start.16 = (bf16[2,2,384,256]{3,2,1,0:T(8,128)(2,1)}, bf16[2,2,384,256]{3,2,1,0:T(8,128)(2,1)}, u32[]{:S(2)}, u32[]{:S(2)}) collective-permute-start(bf16[2,2,384,256]{3,2,1,0:T(8,128)(2,1)} %product.10), channel_id=1, source_target_pairs={{0,2},{1,3},{2,0},{3,1},{4,6},{5,7},{6,4},{7,5},{8,10},{9,11},{10,... | collective-permute-start | bytes 2359304 | tf_op jit(solution)/shard_map/ppermute | solution.py:416
  77.4 8.7 %copy-start.6 = (bf16[256,3072]{1,0:T(8,128)(2,1)}, bf16[256,3072]{1,0:T(8,128)(2,1)S(1)}, u32[]{:S(2)}) copy-start(bf16[256,3072]{1,0:T(8,128)(2,1)S(1)} %collective-permute-done.11.refs_1_) | copy-start | bytes 4718596
  86.1 0.9 copy-start.8
  87.0 11.3 %copy-start.10 = (s32[6]{0:T(128)S(1)}, s32[6]{0:T(128)}, u32[]{:S(2)}) copy-start(s32[6]{0:T(128)} %param.6) | copy-start | bytes 76
  95.3 0.9 copy-start
  98.3 29.1 %collective-permute-start.15 = (bf16[256,3072]{1,0:T(8,128)(2,1)S(1)}, bf16[256,3072]{1,0:T(8,128)(2,1)S(1)}, u32[]{:S(2)}, u32[]{:S(2)}) collective-permute-start(bf16[256,3072]{1,0:T(8,128)(2,1)S(1)} %collective-permute-done.12.refs_0_), channel_id=1, source_target_pairs={{0,1},{1,0},{2,3},{3,2},{4,5},{5,4},{6,7},{7,6},{8,9},{9,8},{10,11... | collective-permute-start | bytes 4718600 | tf_op jit(solution)/shard_map/ppermute | solution.py:422
  98.4 48.4 %collective-permute-start.18 = (bf16[2,2,384,256]{3,2,1,0:T(8,128)(2,1)}, bf16[2,2,384,256]{3,2,1,0:T(8,128)(2,1)S(1)}, u32[]{:S(2)}, u32[]{:S(2)}) collective-permute-start(bf16[2,2,384,256]{3,2,1,0:T(8,128)(2,1)} %copy-done.8), channel_id=1, source_target_pairs={{0,2},{1,3},{2,0},{3,1},{4,6},{5,7},{6,4},{7,5},{8,10},{9,11},{10,... | collective-permute-start | bytes 2359304 | tf_op jit(solution)/shard_map/ppermute | solution.py:416
  99.2 26.5 %copy-start.1 = (f32[1,2,384,256]{3,2,1,0:T(8,128)S(1)}, f32[1,2,384,256]{3,2,1,0:T(8,128)}, u32[]{:S(2)}) copy-start(f32[1,2,384,256]{3,2,1,0:T(8,128)} %copy-done) | copy-start | bytes 2359300
  99.2 26.5 %collective-permute-start.17 = (bf16[1,2,384,256]{3,2,1,0:T(8,128)(2,1)S(1)}, bf16[1,2,384,256]{3,2,1,0:T(8,128)(2,1)S(1)}, u32[]{:S(2)}, u32[]{:S(2)}) collective-permute-start(bf16[1,2,384,256]{3,2,1,0:T(8,128)(2,1)S(1)} %get-tuple-element.75), channel_id=1, source_target_pairs={{0,4},{1,5},{2,6},{3,7},{4,0},{5,1},{6,2},{7,3},{8,12},{9,13},{10,... | collective-permute-start | bytes 1179656 | tf_op jit(solution)/shard_map/ppermute | solution.py:416
  101.4 1.4 copy-start.5
  113.6 44.5 %collective-permute-start.20 = (bf16[1,2,384,256]{3,2,1,0:T(8,128)(2,1)S(1)}, bf16[1,2,384,256]{3,2,1,0:T(8,128)(2,1)S(1)}, u32[]{:S(2)}, u32[]{:S(2)}) collective-permute-start(bf16[1,2,384,256]{3,2,1,0:T(8,128)(2,1)S(1)} %get-tuple-element.83), channel_id=1, source_target_pairs={{0,4},{1,5},{2,6},{3,7},{4,0},{5,1},{6,2},{7,3},{8,12},{9,13},{10,... | collective-permute-start | bytes 1179656 | tf_op jit(solution)/shard_map/ppermute | solution.py:416
  127.4 19.5 %copy-start.3 = (bf16[256,3072]{1,0:T(8,128)(2,1)S(1)}, bf16[256,3072]{1,0:T(8,128)(2,1)}, u32[]{:S(2)}) copy-start(bf16[256,3072]{1,0:T(8,128)(2,1)} %copy-done.2) | copy-start | bytes 4718596
  127.4 19.5 %copy-start.7 = (bf16[256,3072]{1,0:T(8,128)(2,1)S(1)}, bf16[256,3072]{1,0:T(8,128)(2,1)}, u32[]{:S(2)}) copy-start(bf16[256,3072]{1,0:T(8,128)(2,1)} %copy-done.6) | copy-start | bytes 4718596
  141.9 17.9 %collective-permute-start.19 = (bf16[1,2,384,256]{3,2,1,0:T(8,128)(2,1)S(1)}, bf16[1,2,384,256]{3,2,1,0:T(8,128)(2,1)S(1)}, u32[]{:S(2)}, u32[]{:S(2)}) collective-permute-start(bf16[1,2,384,256]{3,2,1,0:T(8,128)(2,1)S(1)} %get-tuple-element.81), channel_id=1, source_target_pairs={{0,2},{1,3},{2,0},{3,1},{4,6},{5,7},{6,4},{7,5},{8,10},{9,11},{10,... | collective-permute-start | bytes 1179656 | tf_op jit(solution)/shard_map/ppermute | solution.py:416
  144.9 20.5 %collective-permute-start.21 = (bf16[1,2,384,256]{3,2,1,0:T(8,128)(2,1)S(1)}, bf16[1,2,384,256]{3,2,1,0:T(8,128)(2,1)S(1)}, u32[]{:S(2)}, u32[]{:S(2)}) collective-permute-start(bf16[1,2,384,256]{3,2,1,0:T(8,128)(2,1)S(1)} %get-tuple-element.85), channel_id=1, source_target_pairs={{0,6},{1,7},{2,4},{3,5},{4,2},{5,3},{6,0},{7,1},{8,14},{9,15},{10,... | collective-permute-start | bytes 1179656 | tf_op jit(solution)/shard_map/ppermute | solution.py:416
  146.8 43.4 %collective-permute-start.22 = (bf16[1,2,384,256]{3,2,1,0:T(8,128)(2,1)S(1)}, bf16[1,2,384,256]{3,2,1,0:T(8,128)(2,1)S(1)}, u32[]{:S(2)}, u32[]{:S(2)}) collective-permute-start(bf16[1,2,384,256]{3,2,1,0:T(8,128)(2,1)S(1)} %get-tuple-element.86), channel_id=1, source_target_pairs={{0,4},{1,5},{2,6},{3,7},{4,0},{5,1},{6,2},{7,3},{8,12},{9,13},{10,... | collective-permute-start | bytes 1179656 | tf_op jit(solution)/shard_map/ppermute | solution.py:416
  155.2 41.7 %collective-permute-start.23 = (bf16[1,2,384,256]{3,2,1,0:T(8,128)(2,1)S(1)}, bf16[1,2,384,256]{3,2,1,0:T(8,128)(2,1)S(1)}, u32[]{:S(2)}, u32[]{:S(2)}) collective-permute-start(bf16[1,2,384,256]{3,2,1,0:T(8,128)(2,1)S(1)} %get-tuple-element.88), channel_id=1, source_target_pairs={{0,4},{1,5},{2,6},{3,7},{4,0},{5,1},{6,2},{7,3},{8,12},{9,13},{10,... | collective-permute-start | bytes 1179656 | tf_op jit(solution)/shard_map/ppermute | solution.py:416
